TPU v7x, 32 devices: a whole 2x2x4 slice. The times are simulated.
32 devices in a mesh: groups: 2 (over x), section: 16 (over z, y, core).
Axes of the slice: x: 2, y: 2, z: 4, core: 2. Of those that a mesh axis runs over, the one named last changes fastest.
Arguments:
- latent_rows: bfloat16 [32, 256, 1408], P(('groups', 'section')), parts along dimension 0, may hold values from -6 to 6
- skip_queue: bfloat16 [32, 256, 1408], P(('groups', 'section')), parts along dimension 0, may hold values from -6 to 6
- norm_gain: float32 [16, 1408], P('section'), may hold values from 0.1 to 1.9
- skip_weight: bfloat16 [16, 2816, 1408], P('section'), may hold values from -0.109375 to 0.109375
- up_weight: bfloat16 [16, 1408, 3072], P('section'), may hold values from -0.15625 to 0.15625
- down_weight: bfloat16 [16, 3072, 1408], P('section'), may hold values from -0.109375 to 0.109375
Outputs:
- next_rows: bfloat16 [32, 256, 1408], P(('groups', 'section')), parts along dimension 0
- next_queue: bfloat16 [32, 256, 1408], P(('groups', 'section')), parts along dimension 0
There are 2 independent parts, one for each index of `groups`. A program takes and returns all parts, laid end to end along the dimension named above; an argument that names none is the same for every part. Nothing has to cross between parts.
All inputs are finite; a program needn't handle non-finite values.
Results may differ from a plain program's by a relative error of at most 0.008.
Values may be sent and summed in bfloat16 or wider, within the bound.
No kernel may reach another device: no remote copies, remote signals or barrier semaphores. Data moves between devices by JAX's collectives and lax.ppermute only.
A program may use at most 128 MiB of HBM per device.

v0:
```python
import jax
import jax.numpy as jnp
from jax import lax
from jax.sharding import PartitionSpec as P

TICKS = 3


epsilon = 1e-06


def from_behind(value, axis, steps):
    count = lax.axis_size(axis)
    pairs = [(source, (source + steps) % count) for source in range(count)]
    return lax.ppermute(value, axis, pairs)


def local(latent_rows, skip_queue, norm_gain, skip_weight, up_weight, down_weight):
    sections = lax.axis_size("section")
    halfway = sections // 2
    position = lax.axis_index("section")
    decoder = position >= halfway
    current = latent_rows[0]
    queue_now = skip_queue[0]
    gain = norm_gain[0]
    merging = skip_weight[0]
    upper = up_weight[0]
    lower = down_weight[0]
    row_count = current.shape[0]
    width = current.shape[1]
    for repeat in range(TICKS):
        incoming = current
        compute_waiting = queue_now

        def with_skip():
            joined = jnp.concatenate([incoming, compute_waiting], axis=1)
            return jnp.dot(joined, merging, preferred_element_type=jnp.float32)

        def without_skip():
            return incoming.astype(jnp.float32)

        merged = lax.cond(decoder, with_skip, without_skip)
        center = jnp.mean(merged, axis=1, keepdims=True)
        spread = jnp.mean(jnp.square(merged - center), axis=1, keepdims=True)
        normed = ((merged - center) * lax.rsqrt(spread + epsilon) * gain).astype(jnp.bfloat16)
        hidden = jax.nn.gelu(
            jnp.dot(normed, upper, preferred_element_type=jnp.float32), approximate=True
        ).astype(jnp.bfloat16)
        output = (merged + jnp.dot(hidden, lower, preferred_element_type=jnp.float32)).astype(
            jnp.bfloat16
        )
        pieces = queue_now.reshape(sections, row_count // sections, width)
        spread_out = lax.all_to_all(pieces, "section", split_axis=0, concat_axis=0, tiled=True)
        targets = jnp.arange(sections, dtype=jnp.int32)
        sources = jnp.where(targets >= halfway, sections - 1 - targets, targets)
        picked = jnp.take(spread_out, sources, axis=0)
        gathered = lax.all_to_all(picked, "section", split_axis=0, concat_axis=0, tiled=True)
        arrived = gathered.reshape(row_count, width)
        current = from_behind(output, "section", 1)
        queue_now = jnp.where(decoder, arrived, output)
    return (current[None], queue_now[None])


def solution(mesh):
    return jax.shard_map(
        local,
        mesh=mesh,
        in_specs=(
            P(("groups", "section"), None, None),
            P(("groups", "section"), None, None),
            P("section", None),
            P("section", None, None),
            P("section", None, None),
            P("section", None, None),
        ),
        out_specs=(P(("groups", "section"), None, None), P(("groups", "section"), None, None)),
        check_vma=False,
    )
```

profile of v0, /device:TPU:16, one launch (start us, length us, event | category | flops | bytes accessed | tf_op | source)
XLA Modules:
  0.0 223.0 jit_solution(12961098846232200606)
XLA Ops:
  0.6 0.0 copy-start
  0.6 0.0 copy-start.1
  0.6 6.3 %all-to-all-start = ((bf16[16,16,1408]{2,1,0:T(8,128)(2,1)}), bf16[16,16,1408]{2,1,0:T(8,128)(2,1)S(1)}, u32[]{:S(2)}, u32[]{:S(2)}) async-start(bf16[16,16,1408]{2,1,0:T(8,128)(2,1)} %bitcast.73), calls=%async_computation | async-start | bytes 1441792 | tf_op jit(solution)/shard_map/all_to_all | solution.py:53
  7.0 18.1 %all-to-all-done = bf16[16,16,1408]{2,1,0:T(8,128)(2,1)S(1)} async-done(((bf16[16,16,1408]{2,1,0:T(8,128)(2,1)}), bf16[16,16,1408]{2,1,0:T(8,128)(2,1)S(1)}, u32[]{:S(2)}, u32[]{:S(2)}) %all-to-all-start) | async-done | bytes 720928 | tf_op jit(solution)/shard_map/all_to_all | solution.py:53
  25.1 0.7 gather_fusion
  25.8 1.0 broadcast_select_fusion.2
  26.8 4.6 %all-to-all-start.1 = ((bf16[16,16,1408]{2,1,0:T(8,128)(2,1)}), bf16[16,16,1408]{2,1,0:T(8,128)(2,1)}, u32[]{:S(2)}, u32[]{:S(2)}) async-start(bf16[16,16,1408]{2,1,0:T(8,128)(2,1)} %broadcast_select_fusion.2), calls=%async_computation.1 | async-start | bytes 1441792 | tf_op jit(solution)/shard_map/all_to_all | solution.py:57
  31.4 0.0 copy-done
  31.4 0.0 copy-done.1
  31.4 0.0 copy-start.4
  31.5 5.7 %conditional.3 = (f32[256,1408]{1,0:T(8,128)S(1)}) conditional(s32[]{:T(128)} %convert_element_type.41, bf16[256,1408]{1,0:T(8,128)(2,1)S(1)} %bitcast.75, (bf16[1,256,1408]{2,1,0:T(8,128)(2,1)S(1)}, bf16[256,1408]{1,0:T(8,128)(2,1)S(1)}, bf16[2816,1408]{1,0:T(8,128)(2,1)}) %tuple.74), branch_computations={%region_0.0_spmd, %region_1.0_spmd} | conditional | flops 2032926720 | bytes 10813448 | solution.py:42
  31.5 5.7 %fusion = f32[256,1408]{1,0:T(8,128)S(1)} fusion(bf16[2816,1408]{1,0:T(8,128)(2,1)} %get-tuple-element.46, bf16[256,1408]{1,0:T(8,128)(2,1)S(1)} %bitcast.74, bf16[256,1408]{1,0:T(8,128)(2,1)S(1)} %get-tuple-element.44), kind=kOutput, calls=%fused_computation.3 | convolution fusion | flops 2032926720 | bytes 10813440 | tf_op jit(solution)/shard_map/cond/branch_1_fun/dot_general | solution.py:37
  37.2 0.2 reduce_sum.72
  37.3 0.0 copy-done.4
  37.4 0.3 multiply_reduce_fusion.2
  37.7 12.0 %all-to-all-done.1 = bf16[16,16,1408]{2,1,0:T(8,128)(2,1)} async-done(((bf16[16,16,1408]{2,1,0:T(8,128)(2,1)}), bf16[16,16,1408]{2,1,0:T(8,128)(2,1)}, u32[]{:S(2)}, u32[]{:S(2)}) %all-to-all-start.1) | async-done | bytes 720928 | tf_op jit(solution)/shard_map/all_to_all | solution.py:57
  49.7 12.2 %bitcast_select_fusion.2 = (bf16[256,1408]{1,0:T(8,128)(2,1)S(1)}, bf16[256,1408]{1,0:T(8,128)(2,1)}) fusion(bf16[16,16,1408]{2,1,0:T(8,128)(2,1)} %all-to-all-done.1, pred[]{:T(512)S(6)} %ge.16, f32[256,1408]{1,0:T(8,128)S(1)} %get-tuple-element.65, bf16[1,3072,1408]{2,1,0:T(8,128)(2,1)} %param.19, bf16[1,1408,3072]{2,1,0:T(8,128)(2,1)} %param.18, ...), kind=kOutput, calls=%fused_computation.71 | convolution fusion | flops 4438786048 | bytes 20913664 | tf_op jit(solution)/shard_map/dot_general | solution.py:49
  61.9 22.7 %all_to_all.30 = bf16[16,16,1408]{2,1,0:T(8,128)(2,1)S(1)} all-to-all(bf16[16,16,1408]{2,1,0:T(8,128)(2,1)S(1)} %bitcast.78), channel_id=1, replica_groups=mesh['groups'=2,'section'=16] {'section'}, dimensions={0} | all-to-all | bytes 1441792 | tf_op jit(solution)/shard_map/all_to_all | solution.py:53
  84.6 0.7 gather_fusion.1
  85.2 1.0 broadcast_select_fusion.1
  86.2 4.7 %all-to-all-start.3 = ((bf16[16,16,1408]{2,1,0:T(8,128)(2,1)}), bf16[16,16,1408]{2,1,0:T(8,128)(2,1)S(1)}, u32[]{:S(2)}, u32[]{:S(2)}) async-start(bf16[16,16,1408]{2,1,0:T(8,128)(2,1)} %broadcast_select_fusion.1), calls=%async_computation.3 | async-start | bytes 1441792 | tf_op jit(solution)/shard_map/all_to_all | solution.py:57
  90.9 0.0 copy-done.6
  90.9 0.2 collective-permute-start
  91.1 25.8 %collective-permute-done = bf16[256,1408]{1,0:T(8,128)(2,1)S(1)} collective-permute-done((bf16[256,1408]{1,0:T(8,128)(2,1)S(1)}, bf16[256,1408]{1,0:T(8,128)(2,1)S(1)}, u32[]{:S(2)}, u32[]{:S(2)}) %collective-permute-start) | collective-permute-done | bytes 720928 | tf_op jit(solution)/shard_map/ppermute | solution.py:15
  116.9 6.9 %conditional.4 = (f32[256,1408]{1,0:T(8,128)S(1)}) conditional(s32[]{:T(128)} %convert_element_type.41, bf16[256,1408]{1,0:T(8,128)(2,1)S(1)} %collective-permute-done, (bf16[256,1408]{1,0:T(8,128)(2,1)S(1)}, bf16[256,1408]{1,0:T(8,128)(2,1)S(1)}, bf16[2816,1408]{1,0:T(8,128)(2,1)}) %tuple.75), branch_computations={%region_4.0_spmd, %region_5.7_spmd} | conditional | flops 2032926720 | bytes 13697060 | solution.py:42
  116.9 0.9 copy-done.3
  117.7 5.9 %fusion.5 = f32[256,1408]{1,0:T(8,128)S(1)} fusion(bf16[2816,1408]{1,0:T(8,128)(2,1)} %get-tuple-element.49, bf16[256,1408]{1,0:T(8,128)(2,1)S(1)} %get-tuple-element.48, bf16[256,1408]{1,0:T(8,128)(2,1)} %copy-done.3), kind=kOutput, calls=%fused_computation.8 | convolution fusion | flops 2032926720 | bytes 10813440 | tf_op jit(solution)/shard_map/cond/branch_1_fun/dot_general | solution.py:37
  123.8 0.2 reduce_sum.74
  124.0 0.3 multiply_reduce_fusion.1
  124.3 0.0 all-to-all-done.3
  124.3 12.1 %bitcast_select_fusion.1 = (bf16[256,1408]{1,0:T(8,128)(2,1)S(1)}, bf16[256,1408]{1,0:T(8,128)(2,1)}) fusion(bf16[16,16,1408]{2,1,0:T(8,128)(2,1)S(1)} %all-to-all-done.3, pred[]{:T(512)S(6)} %ge.16, f32[256,1408]{1,0:T(8,128)S(1)} %get-tuple-element.66, bf16[1,3072,1408]{2,1,0:T(8,128)(2,1)} %param.19, bf16[1,1408,3072]{2,1,0:T(8,128)(2,1)} %param.18, ...), kind=kOutput, calls=%fused_computation.70 | convolution fusion | flops 4438786048 | bytes 20913664 | tf_op jit(solution)/shard_map/dot_general | solution.py:49
  136.4 22.2 %all_to_all.31 = bf16[16,16,1408]{2,1,0:T(8,128)(2,1)S(1)} all-to-all(bf16[16,16,1408]{2,1,0:T(8,128)(2,1)S(1)} %bitcast.77), channel_id=1, replica_groups=mesh['groups'=2,'section'=16] {'section'}, dimensions={0} | all-to-all | bytes 1441792 | tf_op jit(solution)/shard_map/all_to_all | solution.py:53
  158.6 0.7 gather_fusion.2
  159.3 1.0 broadcast_select_fusion
  160.3 4.7 %all-to-all-start.5 = ((bf16[16,16,1408]{2,1,0:T(8,128)(2,1)}), bf16[16,16,1408]{2,1,0:T(8,128)(2,1)S(1)}, u32[]{:S(2)}, u32[]{:S(2)}) async-start(bf16[16,16,1408]{2,1,0:T(8,128)(2,1)} %broadcast_select_fusion), calls=%async_computation.5 | async-start | bytes 1441792 | tf_op jit(solution)/shard_map/all_to_all | solution.py:57
  165.0 0.0 copy-done.5
  165.0 0.2 collective-permute-start.1
  165.2 25.8 %collective-permute-done.1 = bf16[256,1408]{1,0:T(8,128)(2,1)S(1)} collective-permute-done((bf16[256,1408]{1,0:T(8,128)(2,1)S(1)}, bf16[256,1408]{1,0:T(8,128)(2,1)S(1)}, u32[]{:S(2)}, u32[]{:S(2)}) %collective-permute-start.1) | collective-permute-done | bytes 720928 | tf_op jit(solution)/shard_map/ppermute | solution.py:15
  190.9 7.0 %conditional.5 = (f32[256,1408]{1,0:T(8,128)S(1)}) conditional(s32[]{:T(128)} %convert_element_type.41, bf16[256,1408]{1,0:T(8,128)(2,1)S(1)} %collective-permute-done.1, (bf16[256,1408]{1,0:T(8,128)(2,1)S(1)}, bf16[256,1408]{1,0:T(8,128)(2,1)S(1)}, bf16[2816,1408]{1,0:T(8,128)(2,1)}) %tuple.76), branch_computations={%region_8.10_spmd, %region_9.11_spmd} | conditional | flops 2032926720 | bytes 13697060 | solution.py:42
  190.9 0.9 copy-done.2
  191.8 5.9 %fusion.10 = f32[256,1408]{1,0:T(8,128)S(1)} fusion(bf16[2816,1408]{1,0:T(8,128)(2,1)} %get-tuple-element.52, bf16[256,1408]{1,0:T(8,128)(2,1)S(1)} %get-tuple-element.51, bf16[256,1408]{1,0:T(8,128)(2,1)} %copy-done.2), kind=kOutput, calls=%fused_computation.13 | convolution fusion | flops 2032926720 | bytes 10813440 | tf_op jit(solution)/shard_map/cond/branch_1_fun/dot_general | solution.py:37
  197.9 0.2 reduce_sum.76
  198.1 0.3 multiply_reduce_fusion
  198.4 0.0 all-to-all-done.5
  198.4 12.1 %bitcast_select_fusion = (bf16[256,1408]{1,0:T(8,128)(2,1)}, bf16[256,1408]{1,0:T(8,128)(2,1)S(1)}) fusion(bf16[16,16,1408]{2,1,0:T(8,128)(2,1)S(1)} %all-to-all-done.5, pred[]{:T(512)S(6)} %ge.16, f32[256,1408]{1,0:T(8,128)S(1)} %get-tuple-element.67, bf16[1,3072,1408]{2,1,0:T(8,128)(2,1)} %param.19, bf16[1,1408,3072]{2,1,0:T(8,128)(2,1)} %param.18, ...), kind=kOutput, calls=%fused_computation.69 | convolution fusion | flops 4438786048 | bytes 20913664 | tf_op jit(solution)/shard_map/dot_general | solution.py:49
  210.5 0.0 collective-permute-start.2
  210.5 11.6 %collective-permute-done.2 = bf16[256,1408]{1,0:T(8,128)(2,1)S(1)} collective-permute-done((bf16[256,1408]{1,0:T(8,128)(2,1)S(1)}, bf16[256,1408]{1,0:T(8,128)(2,1)S(1)}, u32[]{:S(2)}, u32[]{:S(2)}) %collective-permute-start.2) | collective-permute-done | bytes 720928 | tf_op jit(solution)/shard_map/ppermute | solution.py:15
  222.1 0.9 copy.15
  (14 shorter events, 0.1 us)
Async XLA Ops:
  0.6 30.8 %copy-start = (bf16[1,256,1408]{2,1,0:T(8,128)(2,1)S(1)}, bf16[1,256,1408]{2,1,0:T(8,128)(2,1)}, u32[]{:S(2)}) copy-start(bf16[1,256,1408]{2,1,0:T(8,128)(2,1)} %param.15) | copy-start | bytes 2162692
  0.6 30.8 %copy-start.1 = (bf16[1,256,1408]{2,1,0:T(8,128)(2,1)S(1)}, bf16[1,256,1408]{2,1,0:T(8,128)(2,1)}, u32[]{:S(2)}) copy-start(bf16[1,256,1408]{2,1,0:T(8,128)(2,1)} %param.14) | copy-start | bytes 2162692
  0.6 24.5 %all-to-all-start = ((bf16[16,16,1408]{2,1,0:T(8,128)(2,1)}), bf16[16,16,1408]{2,1,0:T(8,128)(2,1)S(1)}, u32[]{:S(2)}, u32[]{:S(2)}) async-start(bf16[16,16,1408]{2,1,0:T(8,128)(2,1)} %bitcast.73), calls=%async_computation | async-start | bytes 1441792 | tf_op jit(solution)/shard_map/all_to_all | solution.py:53
  26.8 22.9 %all-to-all-start.1 = ((bf16[16,16,1408]{2,1,0:T(8,128)(2,1)}), bf16[16,16,1408]{2,1,0:T(8,128)(2,1)}, u32[]{:S(2)}, u32[]{:S(2)}) async-start(bf16[16,16,1408]{2,1,0:T(8,128)(2,1)} %broadcast_select_fusion.2), calls=%async_computation.1 | async-start | bytes 1441792 | tf_op jit(solution)/shard_map/all_to_all | solution.py:57
  31.4 5.9 %copy-start.4 = (f32[1,1408]{1,0:T(1,128)S(1)}, f32[1,1408]{1,0:T(1,128)}, u32[]{:S(2)}) copy-start(f32[1,1408]{1,0:T(1,128)} %param.16) | copy-start | bytes 16900
  61.9 29.0 %copy-start.6 = (bf16[256,1408]{1,0:T(8,128)(2,1)S(1)}, bf16[256,1408]{1,0:T(8,128)(2,1)}, u32[]{:S(2)}) copy-start(bf16[256,1408]{1,0:T(8,128)(2,1)} %get-tuple-element.56) | copy-start | bytes 2162692
  86.2 38.0 %all-to-all-start.3 = ((bf16[16,16,1408]{2,1,0:T(8,128)(2,1)}), bf16[16,16,1408]{2,1,0:T(8,128)(2,1)S(1)}, u32[]{:S(2)}, u32[]{:S(2)}) async-start(bf16[16,16,1408]{2,1,0:T(8,128)(2,1)} %broadcast_select_fusion.1), calls=%async_computation.3 | async-start | bytes 1441792 | tf_op jit(solution)/shard_map/all_to_all | solution.py:57
  90.9 26.0 %collective-permute-start = (bf16[256,1408]{1,0:T(8,128)(2,1)S(1)}, bf16[256,1408]{1,0:T(8,128)(2,1)S(1)}, u32[]{:S(2)}, u32[]{:S(2)}) collective-permute-start(bf16[256,1408]{1,0:T(8,128)(2,1)S(1)} %copy-done.6), channel_id=1, source_target_pairs={{0,1},{1,2},{2,3},{3,4},{4,5},{5,6},{6,7},{7,8},{8,9},{9,10},{10,1... | collective-permute-start | bytes 2162696 | tf_op jit(solution)/shard_map/ppermute | solution.py:15
  116.9 0.9 copy-start.3
  136.4 28.6 %copy-start.5 = (bf16[256,1408]{1,0:T(8,128)(2,1)S(1)}, bf16[256,1408]{1,0:T(8,128)(2,1)}, u32[]{:S(2)}) copy-start(bf16[256,1408]{1,0:T(8,128)(2,1)} %get-tuple-element.58) | copy-start | bytes 2162692
  160.3 38.1 %all-to-all-start.5 = ((bf16[16,16,1408]{2,1,0:T(8,128)(2,1)}), bf16[16,16,1408]{2,1,0:T(8,128)(2,1)S(1)}, u32[]{:S(2)}, u32[]{:S(2)}) async-start(bf16[16,16,1408]{2,1,0:T(8,128)(2,1)} %broadcast_select_fusion), calls=%async_computation.5 | async-start | bytes 1441792 | tf_op jit(solution)/shard_map/all_to_all | solution.py:57
  165.0 26.0 %collective-permute-start.1 = (bf16[256,1408]{1,0:T(8,128)(2,1)S(1)}, bf16[256,1408]{1,0:T(8,128)(2,1)S(1)}, u32[]{:S(2)}, u32[]{:S(2)}) collective-permute-start(bf16[256,1408]{1,0:T(8,128)(2,1)S(1)} %copy-done.5), channel_id=1, source_target_pairs={{0,1},{1,2},{2,3},{3,4},{4,5},{5,6},{6,7},{7,8},{8,9},{9,10},{10,1... | collective-permute-start | bytes 2162696 | tf_op jit(solution)/shard_map/ppermute | solution.py:15
  190.9 0.9 copy-start.2
  210.5 11.6 %collective-permute-start.2 = (bf16[256,1408]{1,0:T(8,128)(2,1)S(1)}, bf16[256,1408]{1,0:T(8,128)(2,1)S(1)}, u32[]{:S(2)}, u32[]{:S(2)}) collective-permute-start(bf16[256,1408]{1,0:T(8,128)(2,1)S(1)} %get-tuple-element.60), channel_id=1, source_target_pairs={{0,1},{1,2},{2,3},{3,4},{4,5},{5,6},{6,7},{7,8},{8,9},{9,10},{10,1... | collective-permute-start | bytes 2162696 | tf_op jit(solution)/shard_map/ppermute | solution.py:15
where the time goes:
time: 224 us; the launch traced here: 223 us
  waiting for transfers between devices  93.3 us (42%)
  matrix products  53.9 us (24%)
  blocking collectives  44.9 us (20%)
  starting transfers between devices  20.7 us (9%)
  local copies, waits for them, and re-layouts  4.55 us (2%)
  other arithmetic  4.42 us (2%)
    ppermute x3, waiting for transfers between devices, from_behind(): return lax.ppermute(value, axis, pairs)  63.1 us
    all_to_all x2, blocking collectives, local(): lax.all_to_all(pieces, 'section', split_axis=0, concat_axis=0, tiled=True)  44.9 us
    dot_general x3, matrix products, local(): jnp.dot(hidden, lower, preferred_element_type=jnp.float32)  36.4 us
    all_to_all x1, waiting for transfers between devices, local(): lax.all_to_all(pieces, 'section', split_axis=0, concat_axis=0, tiled=True)  18.1 us
    dot_general x3, matrix products, with_skip(): return jnp.dot(joined, merging, preferred_element_type=jnp.float32)  17.5 us
    all_to_all x3, starting transfers between devices, local(): lax.all_to_all(picked, 'section', split_axis=0, concat_axis=0, tiled=True)  14 us
    all_to_all x3, waiting for transfers between devices, local(): lax.all_to_all(picked, 'section', split_axis=0, concat_axis=0, tiled=True)  12 us
    all_to_all x1, starting transfers between devices, local(): lax.all_to_all(pieces, 'section', split_axis=0, concat_axis=0, tiled=True)  6.33 us
  transfers between devices with their start and end apart: 7, of which 5 were waited for; matrix products, arithmetic and copies ran while one was open for 8% of the time, Pallas kernels for 0%

commit v1 on v0

--- a/solution.py
+++ b/solution.py
@@ -15,6 +15,12 @@
     return lax.ppermute(value, axis, pairs)
 
 
+def to_mirror(value, axis):
+    count = lax.axis_size(axis)
+    pairs = [(source, count - 1 - source) for source in range(count // 2)]
+    return lax.ppermute(value, axis, pairs)
+
+
 def local(latent_rows, skip_queue, norm_gain, skip_weight, up_weight, down_weight):
     sections = lax.axis_size("section")
     halfway = sections // 2
@@ -26,8 +32,6 @@
     merging = skip_weight[0]
     upper = up_weight[0]
     lower = down_weight[0]
-    row_count = current.shape[0]
-    width = current.shape[1]
     for repeat in range(TICKS):
         incoming = current
         compute_waiting = queue_now
@@ -39,6 +43,7 @@
         def without_skip():
             return incoming.astype(jnp.float32)
 
+        arrived = to_mirror(queue_now, "section")
         merged = lax.cond(decoder, with_skip, without_skip)
         center = jnp.mean(merged, axis=1, keepdims=True)
         spread = jnp.mean(jnp.square(merged - center), axis=1, keepdims=True)
@@ -49,13 +54,6 @@
         output = (merged + jnp.dot(hidden, lower, preferred_element_type=jnp.float32)).astype(
             jnp.bfloat16
         )
-        pieces = queue_now.reshape(sections, row_count // sections, width)
-        spread_out = lax.all_to_all(pieces, "section", split_axis=0, concat_axis=0, tiled=True)
-        targets = jnp.arange(sections, dtype=jnp.int32)
-        sources = jnp.where(targets >= halfway, sections - 1 - targets, targets)
-        picked = jnp.take(spread_out, sources, axis=0)
-        gathered = lax.all_to_all(picked, "section", split_axis=0, concat_axis=0, tiled=True)
-        arrived = gathered.reshape(row_count, width)
         current = from_behind(output, "section", 1)
         queue_now = jnp.where(decoder, arrived, output)
     return (current[None], queue_now[None])

time: 224 us -> 151 us (0.67)
  blocking collectives: 44.9 us -> 0 us
  starting transfers between devices: 20.7 us -> 4.09 us
  waiting for transfers between devices: 93.3 us -> 86.7 us
  local copies, waits for them, and re-layouts: 4.55 us -> 1.72 us
    all_to_all x2 -> x0, blocking collectives: 44.9 us -> none  [local(): lax.all_to_all(pieces, 'section', split_axis=0, concat_axis=0, tiled=True)]
    all_to_all x4 -> x0, waiting for transfers between devices: 30.2 us -> none  [the longest x1 18.1 us: local(): lax.all_to_all(pieces, 'section', split_axis=0, concat_axis=0, tiled=True)]
    ppermute x0 -> x3, waiting for transfers between devices: none -> 28.3 us  [to_mirror(): return lax.ppermute(value, axis, pairs)]
    all_to_all x4 -> x0, starting transfers between devices: 20.3 us -> none  [the longest x3 14 us: local(): lax.all_to_all(picked, 'section', split_axis=0, concat_axis=0, tiled=True)]
    ppermute x3, waiting for transfers between devices: 63.1 us -> 58.4 us  [from_behind(): return lax.ppermute(value, axis, pairs)]
    ppermute x0 -> x3, starting transfers between devices: none -> 3.85 us  [to_mirror(): return lax.ppermute(value, axis, pairs)]
  transfers between devices with their start and end apart: 7 -> 6, of which waited for: 5 -> 4; matrix products, arithmetic and copies ran while one was open for 8% -> 30% of each run, Pallas kernels for 0% -> 0%
where the time goes in v1:
time: 151 us; the launch traced here: 150 us
  waiting for transfers between devices  86.7 us (57%)
  matrix products  52.8 us (35%)
  starting transfers between devices  4.09 us (3%)
  other arithmetic  3.95 us (3%)
  local copies, waits for them, and re-layouts  1.72 us (1%)
    ppermute x3, waiting for transfers between devices, from_behind(): return lax.ppermute(value, axis, pairs)  58.4 us
    dot_general x3, matrix products, local(): jnp.dot(hidden, lower, preferred_element_type=jnp.float32)  34.7 us
    ppermute x3, waiting for transfers between devices, to_mirror(): return lax.ppermute(value, axis, pairs)  28.3 us
    dot_general x3, matrix products, with_skip(): return jnp.dot(joined, merging, preferred_element_type=jnp.float32)  18.1 us
    ppermute x3, starting transfers between devices, to_mirror(): return lax.ppermute(value, axis, pairs)  3.85 us
  transfers between devices with their start and end apart: 6, of which 4 were waited for; matrix products, arithmetic and copies ran while one was open for 30% of the time, Pallas kernels for 0%

profile of v1, /device:TPU:16, one launch (start us, length us, event | category | flops | bytes accessed | tf_op | source)
XLA Modules:
  0.0 150.4 jit_solution(5284138552329720226)
XLA Ops:
  0.6 1.3 collective-permute-start.1
  1.9 0.7 reduce
  2.7 6.1 %conditional.3 = (f32[256,1408]{1,0:T(8,128)S(1)}) conditional(s32[]{:T(128)} %convert_element_type.41, bf16[256,1408]{1,0:T(8,128)(2,1)} %bitcast.57, (bf16[256,1408]{1,0:T(8,128)(2,1)}, bf16[256,1408]{1,0:T(8,128)(2,1)}, bf16[2816,1408]{1,0:T(8,128)(2,1)}) %tuple.73), branch_computations={%region_0.0_spmd, %region_1.0_spmd} | conditional | flops 2032926720 | bytes 10813448 | solution.py:47
  2.7 6.1 %fusion = f32[256,1408]{1,0:T(8,128)S(1)} fusion(bf16[2816,1408]{1,0:T(8,128)(2,1)} %get-tuple-element.44, bf16[256,1408]{1,0:T(8,128)(2,1)} %get-tuple-element.43, bf16[256,1408]{1,0:T(8,128)(2,1)} %get-tuple-element.42), kind=kOutput, calls=%fused_computation | convolution fusion | flops 2032926720 | bytes 10813440 | tf_op jit(solution)/shard_map/cond/branch_1_fun/dot_general | solution.py:41
  8.8 0.2 reduce_sum.72
  9.0 0.3 multiply_reduce_fusion.2
  9.3 28.3 %collective-permute-done.1 = bf16[256,1408]{1,0:T(8,128)(2,1)S(1)} collective-permute-done((bf16[256,1408]{1,0:T(8,128)(2,1)}, bf16[256,1408]{1,0:T(8,128)(2,1)S(1)}, u32[]{:S(2)}, u32[]{:S(2)}) %collective-permute-start.1) | collective-permute-done | bytes 720928 | tf_op jit(solution)/shard_map/ppermute | solution.py:21
  37.5 12.1 %broadcast_select_fusion.1 = (bf16[256,1408]{1,0:T(8,128)(2,1)}, bf16[256,1408]{1,0:T(8,128)(2,1)S(1)}) fusion(bf16[256,1408]{1,0:T(8,128)(2,1)S(1)} %collective-permute-done.1, pred[]{:T(512)S(6)} %ge.3, f32[256,1408]{1,0:T(8,128)S(1)} %get-tuple-element.59, bf16[1,3072,1408]{2,1,0:T(8,128)(2,1)} %param.17, bf16[1,1408,3072]{2,1,0:T(8,128)(2,1)} %param.16, ...), kind=kOutput, calls=%fused_computation.77 | convolution fusion | flops 4438786048 | bytes 20913664 | tf_op jit(solution)/shard_map/dot_general | solution.py:54
  49.7 0.1 collective-permute-start
  49.8 1.3 collective-permute-start.3
  51.1 22.4 %collective-permute-done = bf16[256,1408]{1,0:T(8,128)(2,1)S(1)} collective-permute-done((bf16[256,1408]{1,0:T(8,128)(2,1)S(1)}, bf16[256,1408]{1,0:T(8,128)(2,1)S(1)}, u32[]{:S(2)}, u32[]{:S(2)}) %collective-permute-start) | collective-permute-done | bytes 720928 | tf_op jit(solution)/shard_map/ppermute | solution.py:15
  73.5 6.1 %conditional.4 = (f32[256,1408]{1,0:T(8,128)S(1)}) conditional(s32[]{:T(128)} %convert_element_type.41, bf16[256,1408]{1,0:T(8,128)(2,1)S(1)} %collective-permute-done, (bf16[256,1408]{1,0:T(8,128)(2,1)S(1)}, bf16[256,1408]{1,0:T(8,128)(2,1)}, bf16[2816,1408]{1,0:T(8,128)(2,1)}) %tuple.71), branch_computations={%region_4.5_spmd, %region_5.6_spmd} | conditional | flops 2032926720 | bytes 10813448 | solution.py:47
  73.5 5.9 %fusion.5 = f32[256,1408]{1,0:T(8,128)S(1)} fusion(bf16[2816,1408]{1,0:T(8,128)(2,1)} %get-tuple-element.47, bf16[256,1408]{1,0:T(8,128)(2,1)} %get-tuple-element.46, bf16[256,1408]{1,0:T(8,128)(2,1)S(1)} %get-tuple-element.45), kind=kOutput, calls=%fused_computation.5 | convolution fusion | flops 2032926720 | bytes 10813440 | tf_op jit(solution)/shard_map/cond/branch_1_fun/dot_general | solution.py:41
  79.6 0.2 reduce_sum.74
  79.7 0.3 multiply_reduce_fusion.1
  80.0 11.3 %fusion.75 = bf16[256,1408]{1,0:T(8,128)(2,1)S(1)} fusion(f32[256,1408]{1,0:T(8,128)S(1)} %get-tuple-element.60, bf16[1,3072,1408]{2,1,0:T(8,128)(2,1)} %param.17, bf16[1,1408,3072]{2,1,0:T(8,128)(2,1)} %param.16, f32[256]{0:T(256)S(1)} %add_rsqrt_fusion.1, f32[256]{0:T(256)S(1)} %broadcast_multiply_fusion.1, f32[1408]{0:T(1024)S(1)} %reduce), kind=kOutput, calls=%fused_computation.58 | convolution fusion | flops 4438425600 | bytes 19471872 | tf_op jit(solution)/shard_map/dot_general | solution.py:54
  91.3 0.1 collective-permute-start.2
  91.4 0.0 collective-permute-done.3
  91.4 0.9 broadcast_select_fusion
  92.3 1.3 collective-permute-start.5
  93.6 25.4 %collective-permute-done.2 = bf16[256,1408]{1,0:T(8,128)(2,1)S(1)} collective-permute-done((bf16[256,1408]{1,0:T(8,128)(2,1)S(1)}, bf16[256,1408]{1,0:T(8,128)(2,1)S(1)}, u32[]{:S(2)}, u32[]{:S(2)}) %collective-permute-start.2) | collective-permute-done | bytes 720928 | tf_op jit(solution)/shard_map/ppermute | solution.py:15
  119.0 7.2 %conditional.5 = (f32[256,1408]{1,0:T(8,128)S(1)}) conditional(s32[]{:T(128)} %convert_element_type.41, bf16[256,1408]{1,0:T(8,128)(2,1)S(1)} %collective-permute-done.2, (bf16[256,1408]{1,0:T(8,128)(2,1)S(1)}, bf16[256,1408]{1,0:T(8,128)(2,1)}, bf16[2816,1408]{1,0:T(8,128)(2,1)}) %tuple.72), branch_computations={%region_8.9_spmd, %region_9.10_spmd} | conditional | flops 2032926720 | bytes 13697060 | solution.py:47
  119.0 0.0 copy-start
  119.0 0.9 copy-done
  119.8 6.1 %fusion.10 = f32[256,1408]{1,0:T(8,128)S(1)} fusion(bf16[2816,1408]{1,0:T(8,128)(2,1)} %get-tuple-element.50, bf16[256,1408]{1,0:T(8,128)(2,1)} %get-tuple-element.49, bf16[256,1408]{1,0:T(8,128)(2,1)} %copy-done), kind=kOutput, calls=%fused_computation.10 | convolution fusion | flops 2032926720 | bytes 10813440 | tf_op jit(solution)/shard_map/cond/branch_1_fun/dot_general | solution.py:41
  126.2 0.2 reduce_sum.76
  126.3 0.3 multiply_reduce_fusion
  126.6 11.3 %fusion.72 = bf16[256,1408]{1,0:T(8,128)(2,1)S(1)} fusion(f32[256,1408]{1,0:T(8,128)S(1)} %get-tuple-element.61, bf16[1,3072,1408]{2,1,0:T(8,128)(2,1)} %param.17, bf16[1,1408,3072]{2,1,0:T(8,128)(2,1)} %param.16, f32[256]{0:T(256)S(1)} %add_rsqrt_fusion, f32[256]{0:T(256)S(1)} %broadcast_multiply_fusion, f32[1408]{0:T(1024)S(1)} %reduce), kind=kOutput, calls=%fused_computation.57 | convolution fusion | flops 4438425600 | bytes 19471872 | tf_op jit(solution)/shard_map/dot_general | solution.py:54
  137.9 0.1 collective-permute-start.4
  138.0 0.0 collective-permute-done.5
  138.0 0.9 select_bitcast_fusion
  138.9 10.6 %collective-permute-done.4 = bf16[256,1408]{1,0:T(8,128)(2,1)S(1)} collective-permute-done((bf16[256,1408]{1,0:T(8,128)(2,1)S(1)}, bf16[256,1408]{1,0:T(8,128)(2,1)S(1)}, u32[]{:S(2)}, u32[]{:S(2)}) %collective-permute-start.4) | collective-permute-done | bytes 720928 | tf_op jit(solution)/shard_map/ppermute | solution.py:15
  149.6 0.9 copy.15
  (6 shorter events, 0.0 us)
Async XLA Ops:
  0.6 36.9 %collective-permute-start.1 = (bf16[256,1408]{1,0:T(8,128)(2,1)}, bf16[256,1408]{1,0:T(8,128)(2,1)S(1)}, u32[]{:S(2)}, u32[]{:S(2)}) collective-permute-start(bf16[256,1408]{1,0:T(8,128)(2,1)} %bitcast.63), channel_id=1, source_target_pairs={{0,15},{1,14},{2,13},{3,12},{4,11},{5,10},{6,9},{7,8},{16,31},{17,... | collective-permute-start | bytes 2162696 | tf_op jit(solution)/shard_map/ppermute | solution.py:21
  49.7 23.8 %collective-permute-start = (bf16[256,1408]{1,0:T(8,128)(2,1)S(1)}, bf16[256,1408]{1,0:T(8,128)(2,1)S(1)}, u32[]{:S(2)}, u32[]{:S(2)}) collective-permute-start(bf16[256,1408]{1,0:T(8,128)(2,1)S(1)} %get-tuple-element.54), channel_id=1, source_target_pairs={{0,1},{1,2},{2,3},{3,4},{4,5},{5,6},{6,7},{7,8},{8,9},{9,10},{10,1... | collective-permute-start | bytes 2162696 | tf_op jit(solution)/shard_map/ppermute | solution.py:15
  49.8 41.6 %collective-permute-start.3 = (bf16[256,1408]{1,0:T(8,128)(2,1)}, bf16[256,1408]{1,0:T(8,128)(2,1)S(1)}, u32[]{:S(2)}, u32[]{:S(2)}) collective-permute-start(bf16[256,1408]{1,0:T(8,128)(2,1)} %get-tuple-element.53), channel_id=1, source_target_pairs={{0,15},{1,14},{2,13},{3,12},{4,11},{5,10},{6,9},{7,8},{16,31},{17,... | collective-permute-start | bytes 2162696 | tf_op jit(solution)/shard_map/ppermute | solution.py:21
  91.3 27.7 %collective-permute-start.2 = (bf16[256,1408]{1,0:T(8,128)(2,1)S(1)}, bf16[256,1408]{1,0:T(8,128)(2,1)S(1)}, u32[]{:S(2)}, u32[]{:S(2)}) collective-permute-start(bf16[256,1408]{1,0:T(8,128)(2,1)S(1)} %fusion.75), channel_id=1, source_target_pairs={{0,1},{1,2},{2,3},{3,4},{4,5},{5,6},{6,7},{7,8},{8,9},{9,10},{10,1... | collective-permute-start | bytes 2162696 | tf_op jit(solution)/shard_map/ppermute | solution.py:15
  92.3 45.6 %collective-permute-start.5 = (bf16[256,1408]{1,0:T(8,128)(2,1)}, bf16[256,1408]{1,0:T(8,128)(2,1)S(1)}, u32[]{:S(2)}, u32[]{:S(2)}) collective-permute-start(bf16[256,1408]{1,0:T(8,128)(2,1)} %broadcast_select_fusion), channel_id=1, source_target_pairs={{0,15},{1,14},{2,13},{3,12},{4,11},{5,10},{6,9},{7,8},{16,31},{17,... | collective-permute-start | bytes 2162696 | tf_op jit(solution)/shard_map/ppermute | solution.py:21
  119.0 0.9 copy-start
  137.9 11.7 %collective-permute-start.4 = (bf16[256,1408]{1,0:T(8,128)(2,1)S(1)}, bf16[256,1408]{1,0:T(8,128)(2,1)S(1)}, u32[]{:S(2)}, u32[]{:S(2)}) collective-permute-start(bf16[256,1408]{1,0:T(8,128)(2,1)S(1)} %fusion.72), channel_id=1, source_target_pairs={{0,1},{1,2},{2,3},{3,4},{4,5},{5,6},{6,7},{7,8},{8,9},{9,10},{10,1... | collective-permute-start | bytes 2162696 | tf_op jit(solution)/shard_map/ppermute | solution.py:15

commit v2 on v1

v2 whole, which is shorter than its diff:
```python
import functools

import jax
import jax.numpy as jnp
from jax import lax
from jax.experimental import pallas as pl
from jax.experimental.pallas import tpu as pltpu
from jax.sharding import PartitionSpec as P

TICKS = 3


epsilon = 1e-06


def from_behind(value, axis, steps):
    count = lax.axis_size(axis)
    pairs = [(source, (source + steps) % count) for source in range(count)]
    return lax.ppermute(value, axis, pairs)


def to_mirror(value, axis):
    count = lax.axis_size(axis)
    pairs = [(source, count - 1 - source) for source in range(count // 2)]
    return lax.ppermute(value, axis, pairs)


def spans(extent, step):
    return [(start, min(step, extent - start)) for start in range(0, extent, step)]


def tick_kernel(
    rows_hbm, queue_hbm, gain_ref, merging_hbm, upper_hbm, lower_hbm, out_ref,
    rows, queue, merging, upper, lower, merged, total, row_sem, merging_sem, upper_sem, lower_sem,
    *, step,
):
    decoder = lax.axis_index("section") >= lax.axis_size("section") // 2
    width = rows.shape[1]
    merge_spans = [
        (base + start, size) for base in (0, width) for start, size in spans(width, step)
    ]
    hidden_spans = spans(upper.shape[1], step)

    rows_copy = pltpu.make_async_copy(rows_hbm, rows, row_sem.at[0])
    queue_copy = pltpu.make_async_copy(queue_hbm, queue, row_sem.at[1])
    merging_copies = [
        pltpu.make_async_copy(
            merging_hbm.at[pl.ds(start, size), :], merging.at[pl.ds(start, size), :], merging_sem.at[i]
        )
        for i, (start, size) in enumerate(merge_spans)
    ]
    upper_copies = [
        pltpu.make_async_copy(
            upper_hbm.at[:, pl.ds(start, size)], upper.at[:, pl.ds(start, size)], upper_sem.at[i]
        )
        for i, (start, size) in enumerate(hidden_spans)
    ]
    lower_copies = [
        pltpu.make_async_copy(
            lower_hbm.at[pl.ds(start, size), :], lower.at[pl.ds(start, size), :], lower_sem.at[i]
        )
        for i, (start, size) in enumerate(hidden_spans)
    ]

    rows_copy.start()

    @pl.when(decoder)
    def _():
        queue_copy.start()
        for copy in merging_copies:
            copy.start()

    for first, second in zip(upper_copies, lower_copies):
        first.start()
        second.start()

    rows_copy.wait()

    @pl.when(decoder)
    def _():
        queue_copy.wait()
        value = None
        for (start, size), copy in zip(merge_spans, merging_copies):
            copy.wait()
            source = rows if start < width else queue
            part = jnp.dot(
                source[:, pl.ds(start % width, size)], merging[pl.ds(start, size), :],
                preferred_element_type=jnp.float32,
            )
            value = part if value is None else value + part
        merged[...] = value

    @pl.when(jnp.logical_not(decoder))
    def _():
        merged[...] = rows[...].astype(jnp.float32)

    value = merged[...]
    center = jnp.mean(value, axis=1, keepdims=True)
    spread = jnp.mean(jnp.square(value - center), axis=1, keepdims=True)
    normed = ((value - center) * lax.rsqrt(spread + epsilon) * gain_ref[...]).astype(jnp.bfloat16)
    for i, (start, size) in enumerate(hidden_spans):
        upper_copies[i].wait()
        raised = jnp.dot(normed, upper[:, pl.ds(start, size)], preferred_element_type=jnp.float32)
        hidden = jax.nn.gelu(raised, approximate=True).astype(jnp.bfloat16)
        lower_copies[i].wait()
        part = jnp.dot(hidden, lower[pl.ds(start, size), :], preferred_element_type=jnp.float32)
        if i == 0:
            total[...] = merged[...] + part
        elif i < len(hidden_spans) - 1:
            total[...] += part
        else:
            out_ref[...] = (total[...] + part).astype(out_ref.dtype)


def tick(rows, queue, gain, merging, upper, lower):
    row_count, width = rows.shape
    hidden = upper.shape[1]
    step = 512
    merge_count = 2 * len(spans(width, step))
    hidden_count = len(spans(hidden, step))
    anywhere = pl.BlockSpec(memory_space=pl.ANY)
    flops = 2 * row_count * width * (2 * width + 2 * hidden)
    moved = 2 * (2 * width * width + 2 * width * hidden + 3 * row_count * width)
    return pl.pallas_call(
        functools.partial(tick_kernel, step=step),
        out_shape=jax.ShapeDtypeStruct((row_count, width), jnp.bfloat16),
        in_specs=[anywhere, anywhere, pl.BlockSpec(memory_space=pltpu.VMEM), anywhere, anywhere, anywhere],
        out_specs=pl.BlockSpec(memory_space=pltpu.VMEM),
        scratch_shapes=[
            pltpu.VMEM((row_count, width), jnp.bfloat16),
            pltpu.VMEM((row_count, width), jnp.bfloat16),
            pltpu.VMEM(merging.shape, jnp.bfloat16),
            pltpu.VMEM(upper.shape, jnp.bfloat16),
            pltpu.VMEM(lower.shape, jnp.bfloat16),
            pltpu.VMEM((row_count, width), jnp.float32),
            pltpu.VMEM((row_count, width), jnp.float32),
            pltpu.SemaphoreType.DMA((2,)),
            pltpu.SemaphoreType.DMA((merge_count,)),
            pltpu.SemaphoreType.DMA((hidden_count,)),
            pltpu.SemaphoreType.DMA((hidden_count,)),
        ],
        compiler_params=pltpu.CompilerParams(vmem_limit_bytes=48 * 1024 * 1024),
        cost_estimate=pl.CostEstimate(
            flops=flops, bytes_accessed=moved, transcendentals=row_count * hidden
        ),
        name="tick",
    )(rows, queue, gain, merging, upper, lower)


def local(latent_rows, skip_queue, norm_gain, skip_weight, up_weight, down_weight):
    sections = lax.axis_size("section")
    decoder = lax.axis_index("section") >= sections // 2
    current = latent_rows[0]
    waiting = skip_queue[0]
    sent = waiting
    for repeat in range(TICKS):
        arrived = to_mirror(sent, "section")
        output = tick(current, waiting, norm_gain, skip_weight[0], up_weight[0], down_weight[0])
        current = from_behind(output, "section", 1)
        waiting = arrived
        sent = output
    queue_now = jnp.where(decoder, arrived, output)
    return (current[None], queue_now[None])


def solution(mesh):
    return jax.shard_map(
        local,
        mesh=mesh,
        in_specs=(
            P(("groups", "section"), None, None),
            P(("groups", "section"), None, None),
            P("section", None),
            P("section", None, None),
            P("section", None, None),
            P("section", None, None),
        ),
        out_specs=(P(("groups", "section"), None, None), P(("groups", "section"), None, None)),
        check_vma=False,
    )
```

time: 151 us -> 150 us (level)
  matrix products: 52.8 us -> 0 us
  Pallas kernels: 0 us -> 41.6 us
  waiting for transfers between devices: 86.7 us -> 96 us
  other arithmetic: 3.95 us -> 0.94 us
  local copies, waits for them, and re-layouts: 1.72 us -> 3.77 us
    dot_general x6 -> x0, matrix products: 52.8 us -> none  [the longest x3 34.7 us: local(): jnp.dot(hidden, lower, preferred_element_type=jnp.float32)]
    pallas_call x0 -> x3, Pallas kernels: none -> 41.6 us  [tick(): pl.pallas_call(functools.partial(tick_kernel, step=step), out_shape=jax.S...]
    ppermute x3, waiting for transfers between devices: 58.4 us -> 67.5 us  [from_behind(): return lax.ppermute(value, axis, pairs)]
    unnamed x1 -> x9, local copies, waits for them, and re-layouts: 0.86 us -> 3.77 us
  transfers between devices with their start and end apart: 6 -> 6, of which waited for: 4 -> 5; matrix products, arithmetic and copies ran while one was open for 30% -> 1% of each run, Pallas kernels for 0% -> 19%
where the time goes in v2:
time: 150 us; the launch traced here: 148 us
  waiting for transfers between devices  96 us (64%)
  Pallas kernels  41.6 us (28%)
  starting transfers between devices  5.15 us (3%)
  local copies, waits for them, and re-layouts  3.77 us (3%)
    ppermute x3, waiting for transfers between devices, from_behind(): return lax.ppermute(value, axis, pairs)  67.5 us
    pallas_call x3, Pallas kernels, tick(): pl.pallas_call(functools.partial(tick_kernel, step=step), out_shape=jax.S...  41.6 us
    ppermute x3, waiting for transfers between devices, to_mirror(): return lax.ppermute(value, axis, pairs)  28.5 us
    ppermute x3, starting transfers between devices, to_mirror(): return lax.ppermute(value, axis, pairs)  3.88 us
    unnamed x9, local copies, waits for them, and re-layouts  3.77 us
  transfers between devices with their start and end apart: 6, of which 5 were waited for; matrix products, arithmetic and copies ran while one was open for 1% of the time, Pallas kernels for 19%

profile of v2, /device:TPU:16, one launch (start us, length us, event | category | flops | bytes accessed | tf_op | source)
XLA Modules:
  0.0 148.2 jit_solution(15343378786743486837)
XLA Ops:
  0.6 0.0 copy-start
  0.6 1.1 copy-done
  1.7 0.0 copy-start.1
  1.7 1.1 copy-done.1
  2.9 0.0 copy-start.2
  2.9 0.7 copy-done.2
  3.5 13.7 %tick.3 = bf16[256,1408]{1,0:T(8,128)(2,1)S(1)} custom-call(bf16[256,1408]{1,0:T(8,128)(2,1)S(1)} %bitcast.8, bf16[256,1408]{1,0:T(8,128)(2,1)S(1)} %bitcast.9, f32[1,1408]{1,0:T(1,128)S(1)} %copy-done.2, bf16[2816,1408]{1,0:T(8,128)(2,1)} %bitcast.17, bf16[1408,3072]{1,0:T(8,128)(2,1)} %bitcast.11, bf16[3072,1408]{1,0:T(8,128)(2,1)} %bitcast.14), custom_call_target="tpu_custom_call" | custom-call | flops 6459228160 | bytes 27394048 | tf_op jit(solution)/shard_map/tick/pallas_call | solution.py:124
  17.3 0.0 copy-start.3
  17.3 0.1 collective-permute-start
  17.4 1.3 collective-permute-start.1
  18.7 1.3 collective-permute-start.3
  20.0 43.9 %collective-permute-done.rows_hbm = bf16[256,1408]{1,0:T(8,128)(2,1)S(1)} collective-permute-done((bf16[256,1408]{1,0:T(8,128)(2,1)S(1)}, bf16[256,1408]{1,0:T(8,128)(2,1)S(1)}, u32[]{:S(2)}, u32[]{:S(2)}) %collective-permute-start) | collective-permute-done | bytes 720928 | tf_op jit(solution)/shard_map/ppermute | solution.py:19
  63.8 15.4 %collective-permute-done.1.queue_hbm = bf16[256,1408]{1,0:T(8,128)(2,1)S(1)} collective-permute-done((bf16[256,1408]{1,0:T(8,128)(2,1)S(1)}, bf16[256,1408]{1,0:T(8,128)(2,1)S(1)}, u32[]{:S(2)}, u32[]{:S(2)}) %collective-permute-start.1) | collective-permute-done | bytes 720928 | tf_op jit(solution)/shard_map/ppermute | solution.py:25
  79.3 13.9 %tick.4 = bf16[256,1408]{1,0:T(8,128)(2,1)S(1)} custom-call(bf16[256,1408]{1,0:T(8,128)(2,1)S(1)} %collective-permute-done.rows_hbm, bf16[256,1408]{1,0:T(8,128)(2,1)S(1)} %collective-permute-done.1.queue_hbm, f32[1,1408]{1,0:T(1,128)S(1)} %copy-done.2, bf16[2816,1408]{1,0:T(8,128)(2,1)} %bitcast.18, bf16[1408,3072]{1,0:T(8,128)(2,1)} %bitcast.12, ...), custom_call_target="tpu_custom_call" | custom-call | flops 6459228160 | bytes 27394048 | tf_op jit(solution)/shard_map/tick/pallas_call | solution.py:124
  93.2 0.1 collective-permute-start.2
  93.3 1.3 collective-permute-start.5
  94.6 13.0 %collective-permute-done.3.queue_hbm = bf16[256,1408]{1,0:T(8,128)(2,1)S(1)} collective-permute-done((bf16[256,1408]{1,0:T(8,128)(2,1)S(1)}, bf16[256,1408]{1,0:T(8,128)(2,1)S(1)}, u32[]{:S(2)}, u32[]{:S(2)}) %collective-permute-start.3) | collective-permute-done | bytes 720928 | tf_op jit(solution)/shard_map/ppermute | solution.py:25
  107.6 14.0 %collective-permute-done.2.rows_hbm = bf16[256,1408]{1,0:T(8,128)(2,1)S(1)} collective-permute-done((bf16[256,1408]{1,0:T(8,128)(2,1)S(1)}, bf16[256,1408]{1,0:T(8,128)(2,1)S(1)}, u32[]{:S(2)}, u32[]{:S(2)}) %collective-permute-start.2) | collective-permute-done | bytes 720928 | tf_op jit(solution)/shard_map/ppermute | solution.py:19
  121.7 0.0 copy-done.3
  121.7 14.0 %tick.5 = bf16[256,1408]{1,0:T(8,128)(2,1)S(1)} custom-call(bf16[256,1408]{1,0:T(8,128)(2,1)S(1)} %collective-permute-done.2.rows_hbm, bf16[256,1408]{1,0:T(8,128)(2,1)S(1)} %collective-permute-done.3.queue_hbm, f32[1,1408]{1,0:T(1,128)S(1)} %copy-done.3, bf16[2816,1408]{1,0:T(8,128)(2,1)} %bitcast.19, bf16[1408,3072]{1,0:T(8,128)(2,1)} %bitcast.13, ...), custom_call_target="tpu_custom_call" | custom-call | flops 6459228160 | bytes 27394048 | tf_op jit(solution)/shard_map/tick/pallas_call | solution.py:124
  135.6 1.2 collective-permute-start.4
  136.8 0.0 collective-permute-done.5
  136.8 0.9 select_bitcast_fusion
  137.7 9.6 %collective-permute-done.4 = bf16[256,1408]{1,0:T(8,128)(2,1)S(1)} collective-permute-done((bf16[256,1408]{1,0:T(8,128)(2,1)S(1)}, bf16[256,1408]{1,0:T(8,128)(2,1)S(1)}, u32[]{:S(2)}, u32[]{:S(2)}) %collective-permute-start.4) | collective-permute-done | bytes 720928 | tf_op jit(solution)/shard_map/ppermute | solution.py:19
  147.3 0.9 copy.9
Async XLA Ops:
  0.6 1.1 copy-start
  1.7 1.1 copy-start.1
  2.9 0.7 copy-start.2
  17.3 104.4 %copy-start.3 = (f32[1,1408]{1,0:T(1,128)S(1)}, f32[1,1408]{1,0:T(1,128)}, u32[]{:S(2)}) copy-start(f32[1,1408]{1,0:T(1,128)} %gain_ref.5) | copy-start | bytes 16900
  17.3 46.5 %collective-permute-start = (bf16[256,1408]{1,0:T(8,128)(2,1)S(1)}, bf16[256,1408]{1,0:T(8,128)(2,1)S(1)}, u32[]{:S(2)}, u32[]{:S(2)}) collective-permute-start(bf16[256,1408]{1,0:T(8,128)(2,1)S(1)} %tick.3), channel_id=1, source_target_pairs={{0,1},{1,2},{2,3},{3,4},{4,5},{5,6},{6,7},{7,8},{8,9},{9,10},{10,1... | collective-permute-start | bytes 2162696 | tf_op jit(solution)/shard_map/ppermute | solution.py:19
  17.4 61.9 %collective-permute-start.1 = (bf16[256,1408]{1,0:T(8,128)(2,1)S(1)}, bf16[256,1408]{1,0:T(8,128)(2,1)S(1)}, u32[]{:S(2)}, u32[]{:S(2)}) collective-permute-start(bf16[256,1408]{1,0:T(8,128)(2,1)S(1)} %bitcast.10), channel_id=1, source_target_pairs={{0,15},{1,14},{2,13},{3,12},{4,11},{5,10},{6,9},{7,8},{16,31},{17,... | collective-permute-start | bytes 2162696 | tf_op jit(solution)/shard_map/ppermute | solution.py:25
  18.7 88.9 %collective-permute-start.3 = (bf16[256,1408]{1,0:T(8,128)(2,1)S(1)}, bf16[256,1408]{1,0:T(8,128)(2,1)S(1)}, u32[]{:S(2)}, u32[]{:S(2)}) collective-permute-start(bf16[256,1408]{1,0:T(8,128)(2,1)S(1)} %tick.3), channel_id=1, source_target_pairs={{0,15},{1,14},{2,13},{3,12},{4,11},{5,10},{6,9},{7,8},{16,31},{17,... | collective-permute-start | bytes 2162696 | tf_op jit(solution)/shard_map/ppermute | solution.py:25
  93.2 28.5 %collective-permute-start.2 = (bf16[256,1408]{1,0:T(8,128)(2,1)S(1)}, bf16[256,1408]{1,0:T(8,128)(2,1)S(1)}, u32[]{:S(2)}, u32[]{:S(2)}) collective-permute-start(bf16[256,1408]{1,0:T(8,128)(2,1)S(1)} %tick.4), channel_id=1, source_target_pairs={{0,1},{1,2},{2,3},{3,4},{4,5},{5,6},{6,7},{7,8},{8,9},{9,10},{10,1... | collective-permute-start | bytes 2162696 | tf_op jit(solution)/shard_map/ppermute | solution.py:19
  93.3 43.5 %collective-permute-start.5 = (bf16[256,1408]{1,0:T(8,128)(2,1)S(1)}, bf16[256,1408]{1,0:T(8,128)(2,1)S(1)}, u32[]{:S(2)}, u32[]{:S(2)}) collective-permute-start(bf16[256,1408]{1,0:T(8,128)(2,1)S(1)} %tick.4), channel_id=1, source_target_pairs={{0,15},{1,14},{2,13},{3,12},{4,11},{5,10},{6,9},{7,8},{16,31},{17,... | collective-permute-start | bytes 2162696 | tf_op jit(solution)/shard_map/ppermute | solution.py:25
  135.6 11.7 %collective-permute-start.4 = (bf16[256,1408]{1,0:T(8,128)(2,1)S(1)}, bf16[256,1408]{1,0:T(8,128)(2,1)S(1)}, u32[]{:S(2)}, u32[]{:S(2)}) collective-permute-start(bf16[256,1408]{1,0:T(8,128)(2,1)S(1)} %tick.5), channel_id=1, source_target_pairs={{0,1},{1,2},{2,3},{3,4},{4,5},{5,6},{6,7},{7,8},{8,9},{9,10},{10,1... | collective-permute-start | bytes 2162696 | tf_op jit(solution)/shard_map/ppermute | solution.py:19

commit v3 on v1

v3 whole, which is shorter than its diff:
```python
import functools

import jax
import jax.numpy as jnp
from jax import lax
from jax.experimental import pallas as pl
from jax.experimental.pallas import tpu as pltpu
from jax.sharding import PartitionSpec as P

TICKS = 3


epsilon = 1e-06


def move(value, pairs):
    return lax.ppermute(value, "section", pairs)


def spans(extent, step):
    cuts = [0] + list(range(min(step // 2, extent), extent, step)) + [extent]
    return [(start, stop - start) for start, stop in zip(cuts[:-1], cuts[1:])]


def even_spans(extent, step):
    return [(start, min(step, extent - start)) for start in range(0, extent, step)]


def block_kernel(
    *refs, row_sources, queue_sources, role, step, merge_step,
):
    rows_hbm, refs = refs[: len(row_sources)], refs[len(row_sources) :]
    queue_hbm, refs = refs[: len(queue_sources)], refs[len(queue_sources) :]
    (
        gain_ref, merging_hbm, upper_hbm, lower_hbm, after_hbm, out_ref,
        rows, queue, merging, upper, lower, merged, total, row_sem, merging_sem, upper_sem, lower_sem,
    ) = refs
    section = lax.axis_index("section")
    decoder = section >= lax.axis_size("section") // 2
    width = rows.shape[1]
    merge_spans = [(base + start, size) for base in (0, width) for start, size in even_spans(width, merge_step)]
    hidden_spans = spans(upper.shape[1], step)

    row_copies = [pltpu.make_async_copy(source, rows, row_sem.at[0]) for source in rows_hbm]
    queue_copies = [pltpu.make_async_copy(source, queue, row_sem.at[1]) for source in queue_hbm]
    merging_copies = [
        pltpu.make_async_copy(
            merging_hbm.at[pl.ds(start, size), :], merging.at[pl.ds(start, size), :], merging_sem.at[i]
        )
        for i, (start, size) in enumerate(merge_spans)
    ]
    upper_copies = [
        pltpu.make_async_copy(
            upper_hbm.at[:, pl.ds(start, size)], upper.at[:, pl.ds(start, size)], upper_sem.at[i]
        )
        for i, (start, size) in enumerate(hidden_spans)
    ]
    lower_copies = [
        pltpu.make_async_copy(
            lower_hbm.at[pl.ds(start, size), :], lower.at[pl.ds(start, size), :], lower_sem.at[i]
        )
        for i, (start, size) in enumerate(hidden_spans)
    ]

    def start_one(tests, copies):
        for test, copy in zip(tests, copies):
            if test is None:
                copy.start()
            else:
                pl.when(test(section))(copy.start)

    def work():
        start_one(row_sources, row_copies)

        @pl.when(decoder)
        def _():
            if not queue_copies:
                return
            start_one(queue_sources, queue_copies)
            for copy in merging_copies:
                copy.start()

        for first, second in zip(upper_copies, lower_copies):
            first.start()
            second.start()

        row_copies[0].wait()

        @pl.when(decoder)
        def _():
            if not queue_copies:
                return
            queue_copies[0].wait()
            value = None
            for (start, size), copy in zip(merge_spans, merging_copies):
                copy.wait()
                source = rows if start < width else queue
                part = jnp.dot(
                    source[:, pl.ds(start % width, size)], merging[pl.ds(start, size), :],
                    preferred_element_type=jnp.float32,
                )
                value = part if value is None else value + part
            merged[...] = value

        @pl.when(jnp.logical_not(decoder))
        def _():
            merged[...] = rows[...].astype(jnp.float32)

        value = merged[...]
        center = jnp.mean(value, axis=1, keepdims=True)
        spread = jnp.mean(jnp.square(value - center), axis=1, keepdims=True)
        normed = ((value - center) * lax.rsqrt(spread + epsilon) * gain_ref[...]).astype(jnp.bfloat16)
        for i, (start, size) in enumerate(hidden_spans):
            upper_copies[i].wait()
            raised = jnp.dot(normed, upper[:, pl.ds(start, size)], preferred_element_type=jnp.float32)
            hidden = jax.nn.gelu(raised, approximate=True).astype(jnp.bfloat16)
            lower_copies[i].wait()
            part = jnp.dot(hidden, lower[pl.ds(start, size), :], preferred_element_type=jnp.float32)
            if i == 0:
                total[...] = merged[...] + part
            elif i < len(hidden_spans) - 1:
                total[...] += part
            else:
                out_ref[...] = (total[...] + part).astype(out_ref.dtype)

    if role is None:
        work()
    else:
        pl.when(decoder if role == "decoder" else jnp.logical_not(decoder))(work)


def block(row_choices, queue_choices, weights, name, role=None, after=None):
    gain, merging, upper, lower = weights
    row_count, width = row_choices[0][1].shape
    hidden = upper.shape[1]
    step, merge_step = 1024, 512
    anywhere = pl.BlockSpec(memory_space=pl.ANY)
    resident = pl.BlockSpec(memory_space=pltpu.VMEM)
    after = row_choices[0][1] if after is None else after
    arrays = [array for _, array in row_choices] + [array for _, array in queue_choices]
    return pl.pallas_call(
        functools.partial(
            block_kernel,
            row_sources=[test for test, _ in row_choices],
            queue_sources=[test for test, _ in queue_choices],
            role=role, step=step, merge_step=merge_step,
        ),
        out_shape=jax.ShapeDtypeStruct((row_count, width), jnp.bfloat16),
        in_specs=[anywhere] * len(arrays) + [resident, anywhere, anywhere, anywhere, anywhere],
        out_specs=resident,
        scratch_shapes=[
            pltpu.VMEM((row_count, width), jnp.bfloat16),
            pltpu.VMEM((row_count, width), jnp.bfloat16),
            pltpu.VMEM(merging.shape, jnp.bfloat16),
            pltpu.VMEM(upper.shape, jnp.bfloat16),
            pltpu.VMEM(lower.shape, jnp.bfloat16),
            pltpu.VMEM((row_count, width), jnp.float32),
            pltpu.VMEM((row_count, width), jnp.float32),
            pltpu.SemaphoreType.DMA((2,)),
            pltpu.SemaphoreType.DMA((2 * len(even_spans(width, merge_step)),)),
            pltpu.SemaphoreType.DMA((len(spans(hidden, step)),)),
            pltpu.SemaphoreType.DMA((len(spans(hidden, step)),)),
        ],
        compiler_params=pltpu.CompilerParams(vmem_limit_bytes=48 * 1024 * 1024),
        cost_estimate=pl.CostEstimate(
            flops=2 * row_count * width * (2 * width + 2 * hidden),
            bytes_accessed=2 * (merging.size + upper.size + lower.size + 3 * row_count * width),
            transcendentals=row_count * hidden,
        ),
        name=name,
    )(*arrays, gain, merging, upper, lower, after)


def local(latent_rows, skip_queue, norm_gain, skip_weight, up_weight, down_weight):
    count = lax.axis_size("section")
    half = count // 2
    quarter = half // 2
    section = lax.axis_index("section")
    weights = (norm_gain, skip_weight[0], up_weight[0], down_weight[0])
    step_on = [(source, (source + 1) % count) for source in range(count)]
    handed = [(source, source + quarter) for source in range(quarter)]
    direct = [(source, count - 1 - source) for source in range(quarter, half)]
    passed = [(source + quarter, count - 1 - source) for source in range(quarter)]
    is_near = lambda section: section < half + quarter
    is_far = lambda section: section >= half + quarter

    arrived = move(skip_queue[0], handed + direct)
    output = block([(None, latent_rows[0])], [(None, skip_queue[0])], weights, "tick_0")
    for number in range(1, TICKS):
        rows = move(output, step_on)
        arriving = move(output, handed + direct)
        queue = [(is_near, arrived), (is_far, move(arrived, passed))]
        output = block([(None, rows)], queue, weights, "tick_%d" % number)
        arrived = arriving
    rows = move(output, step_on)
    far = move(arrived, passed)
    queue_now = jnp.where(section >= half, jnp.where(is_far(section), far, arrived), output)
    return (rows[None], queue_now[None])


def solution(mesh):
    return jax.shard_map(
        local,
        mesh=mesh,
        in_specs=(
            P(("groups", "section"), None, None),
            P(("groups", "section"), None, None),
            P("section", None),
            P("section", None, None),
            P("section", None, None),
            P("section", None, None),
        ),
        out_specs=(P(("groups", "section"), None, None), P(("groups", "section"), None, None)),
        check_vma=False,
    )
```

time: 151 us -> 133 us (0.88)
  the two profiles are of different devices: /device:TPU:16 before, /device:TPU:24 now
where the time goes in v3:
time: 133 us; the launch traced here: 132 us
  waiting for transfers between devices  80.8 us (61%)
  Pallas kernels  39.7 us (30%)
  starting transfers between devices  6.17 us (5%)
  local copies, waits for them, and re-layouts  3.76 us (3%)
    ppermute x9, waiting for transfers between devices, move(): return lax.ppermute(value, 'section', pairs)  80.8 us
    pallas_call x3, Pallas kernels, block(): pl.pallas_call(functools.partial(block_kernel, row_sources=[test for test...  39.7 us
    ppermute x9, starting transfers between devices, move(): return lax.ppermute(value, 'section', pairs)  6.17 us
    unnamed x9, local copies, waits for them, and re-layouts  3.76 us
  transfers between devices with their start and end apart: 9, of which 4 were waited for; matrix products, arithmetic and copies ran while one was open for 0% of the time, Pallas kernels for 30%

profile of v3, /device:TPU:24, one launch (start us, length us, event | category | flops | bytes accessed | tf_op | source)
XLA Modules:
  0.0 132.2 jit_solution(5043541418209947706)
XLA Ops:
  0.6 0.7 collective-permute-start.1
  1.3 0.0 copy-start
  1.4 1.1 copy-done
  2.5 0.0 copy-start.1
  2.5 1.1 copy-done.1
  3.6 0.0 copy-start.2
  3.6 0.7 copy-done.2
  4.3 0.0 copy-start.3
  4.3 13.1 %tick_0.1 = bf16[256,1408]{1,0:T(8,128)(2,1)S(1)} custom-call(bf16[256,1408]{1,0:T(8,128)(2,1)S(1)} %bitcast.8, bf16[256,1408]{1,0:T(8,128)(2,1)S(1)} %bitcast.11, f32[1,1408]{1,0:T(1,128)S(1)} %copy-done.2, bf16[2816,1408]{1,0:T(8,128)(2,1)} %bitcast.18, bf16[1408,3072]{1,0:T(8,128)(2,1)} %bitcast.12, bf16[3072,1408]{1,0:T(8,128)(2,1)} %bitcast.15, ...), custom_call_target="tpu_custom_call" | custom-call | flops 6459228160 | bytes 27394048 | tf_op jit(solution)/shard_map/tick_0/pallas_call | solution.py:141
  17.4 0.7 collective-permute-start.4
  18.1 0.1 collective-permute-start
  18.2 0.0 collective-permute-done.1.refs_1_
  18.2 1.3 collective-permute-start.2
  19.5 0.0 collective-permute-done.4.refs_1_
  19.5 1.3 collective-permute-start.5
  20.8 9.0 %collective-permute-done.refs_0_.refs_7_ = bf16[256,1408]{1,0:T(8,128)(2,1)S(1)} collective-permute-done((bf16[256,1408]{1,0:T(8,128)(2,1)S(1)}, bf16[256,1408]{1,0:T(8,128)(2,1)S(1)}, u32[]{:S(2)}, u32[]{:S(2)}) %collective-permute-start) | collective-permute-done | bytes 720928 | tf_op jit(solution)/shard_map/ppermute | solution.py:17
  29.8 40.2 %collective-permute-done.2.refs_2_ = bf16[256,1408]{1,0:T(8,128)(2,1)S(1)} collective-permute-done((bf16[256,1408]{1,0:T(8,128)(2,1)S(1)}, bf16[256,1408]{1,0:T(8,128)(2,1)S(1)}, u32[]{:S(2)}, u32[]{:S(2)}) %collective-permute-start.2) | collective-permute-done | bytes 720928 | tf_op jit(solution)/shard_map/ppermute | solution.py:17
  70.0 0.0 copy-done.3
  70.0 13.3 %tick_1.1 = bf16[256,1408]{1,0:T(8,128)(2,1)S(1)} custom-call(bf16[256,1408]{1,0:T(8,128)(2,1)S(1)} %collective-permute-done.refs_0_.refs_7_, bf16[256,1408]{1,0:T(8,128)(2,1)S(1)} %collective-permute-done.1.refs_1_, bf16[256,1408]{1,0:T(8,128)(2,1)S(1)} %collective-permute-done.2.refs_2_, f32[1,1408]{1,0:T(1,128)S(1)} %copy-done.3, ...), custom_call_target="tpu_custom_call" | custom-call | flops 6459228160 | bytes 27394048 | tf_op jit(solution)/shard_map/tick_1/pallas_call | solution.py:141
  83.3 0.1 collective-permute-start.3
  83.3 0.7 collective-permute-start.7
  84.1 0.0 collective-permute-done.5.refs_2_
  84.1 10.9 %collective-permute-done.3.refs_0_.refs_7_ = bf16[256,1408]{1,0:T(8,128)(2,1)S(1)} collective-permute-done((bf16[256,1408]{1,0:T(8,128)(2,1)S(1)}, bf16[256,1408]{1,0:T(8,128)(2,1)S(1)}, u32[]{:S(2)}, u32[]{:S(2)}) %collective-permute-start.3) | collective-permute-done | bytes 720928 | tf_op jit(solution)/shard_map/ppermute | solution.py:17
  94.9 13.3 %tick_2.1 = bf16[256,1408]{1,0:T(8,128)(2,1)S(1)} custom-call(bf16[256,1408]{1,0:T(8,128)(2,1)S(1)} %collective-permute-done.3.refs_0_.refs_7_, bf16[256,1408]{1,0:T(8,128)(2,1)S(1)} %collective-permute-done.4.refs_1_, bf16[256,1408]{1,0:T(8,128)(2,1)S(1)} %collective-permute-done.5.refs_2_, f32[1,1408]{1,0:T(1,128)S(1)} %copy-done.3, ...), custom_call_target="tpu_custom_call" | custom-call | flops 6459228160 | bytes 27394048 | tf_op jit(solution)/shard_map/tick_2/pallas_call | solution.py:141
  108.3 0.1 collective-permute-start.6
  108.3 0.0 collective-permute-done.7
  108.4 1.3 collective-permute-start.8
  109.7 20.7 %collective-permute-done.6 = bf16[256,1408]{1,0:T(8,128)(2,1)S(1)} collective-permute-done((bf16[256,1408]{1,0:T(8,128)(2,1)S(1)}, bf16[256,1408]{1,0:T(8,128)(2,1)S(1)}, u32[]{:S(2)}, u32[]{:S(2)}) %collective-permute-start.6) | collective-permute-done | bytes 720928 | tf_op jit(solution)/shard_map/ppermute | solution.py:17
  130.4 0.0 collective-permute-done.8
  130.4 1.0 select_bitcast_fusion
  131.3 0.9 copy.9
Async XLA Ops:
  0.6 17.5 %collective-permute-start.1 = (bf16[256,1408]{1,0:T(8,128)(2,1)}, bf16[256,1408]{1,0:T(8,128)(2,1)S(1)}, u32[]{:S(2)}, u32[]{:S(2)}) collective-permute-start(bf16[256,1408]{1,0:T(8,128)(2,1)} %bitcast.10), channel_id=1, source_target_pairs={{0,4},{1,5},{2,6},{3,7},{4,11},{5,10},{6,9},{7,8},{16,20},{17,21},... | collective-permute-start | bytes 2162696 | tf_op jit(solution)/shard_map/ppermute | solution.py:17
  1.3 1.1 copy-start
  2.5 1.1 copy-start.1
  3.6 0.7 copy-start.2
  4.3 65.7 %copy-start.3 = (f32[1,1408]{1,0:T(1,128)S(1)}, f32[1,1408]{1,0:T(1,128)}, u32[]{:S(2)}) copy-start(f32[1,1408]{1,0:T(1,128)} %refs_3_.3) | copy-start | bytes 16900
  17.4 2.1 %collective-permute-start.4 = (bf16[256,1408]{1,0:T(8,128)(2,1)S(1)}, bf16[256,1408]{1,0:T(8,128)(2,1)S(1)}, u32[]{:S(2)}, u32[]{:S(2)}) collective-permute-start(bf16[256,1408]{1,0:T(8,128)(2,1)S(1)} %tick_0.1), channel_id=1, source_target_pairs={{0,4},{1,5},{2,6},{3,7},{4,11},{5,10},{6,9},{7,8},{16,20},{17,21},... | collective-permute-start | bytes 2162696 | tf_op jit(solution)/shard_map/ppermute | solution.py:17
  18.1 11.7 %collective-permute-start = (bf16[256,1408]{1,0:T(8,128)(2,1)S(1)}, bf16[256,1408]{1,0:T(8,128)(2,1)S(1)}, u32[]{:S(2)}, u32[]{:S(2)}) collective-permute-start(bf16[256,1408]{1,0:T(8,128)(2,1)S(1)} %tick_0.1), channel_id=1, source_target_pairs={{0,1},{1,2},{2,3},{3,4},{4,5},{5,6},{6,7},{7,8},{8,9},{9,10},{10,1... | collective-permute-start | bytes 2162696 | tf_op jit(solution)/shard_map/ppermute | solution.py:17
  18.2 51.8 %collective-permute-start.2 = (bf16[256,1408]{1,0:T(8,128)(2,1)S(1)}, bf16[256,1408]{1,0:T(8,128)(2,1)S(1)}, u32[]{:S(2)}, u32[]{:S(2)}) collective-permute-start(bf16[256,1408]{1,0:T(8,128)(2,1)S(1)} %collective-permute-done.1.refs_1_), channel_id=1, source_target_pairs={{4,15},{5,14},{6,13},{7,12},{20,31},{21,30},{22,29},{23,28}} | collective-permute-start | bytes 2162696 | tf_op jit(solution)/shard_map/ppermute | solution.py:17
  19.5 64.6 %collective-permute-start.5 = (bf16[256,1408]{1,0:T(8,128)(2,1)S(1)}, bf16[256,1408]{1,0:T(8,128)(2,1)S(1)}, u32[]{:S(2)}, u32[]{:S(2)}) collective-permute-start(bf16[256,1408]{1,0:T(8,128)(2,1)S(1)} %collective-permute-done.4.refs_1_), channel_id=1, source_target_pairs={{4,15},{5,14},{6,13},{7,12},{20,31},{21,30},{22,29},{23,28}} | collective-permute-start | bytes 2162696 | tf_op jit(solution)/shard_map/ppermute | solution.py:17
  83.3 11.7 %collective-permute-start.3 = (bf16[256,1408]{1,0:T(8,128)(2,1)S(1)}, bf16[256,1408]{1,0:T(8,128)(2,1)S(1)}, u32[]{:S(2)}, u32[]{:S(2)}) collective-permute-start(bf16[256,1408]{1,0:T(8,128)(2,1)S(1)} %tick_1.1), channel_id=1, source_target_pairs={{0,1},{1,2},{2,3},{3,4},{4,5},{5,6},{6,7},{7,8},{8,9},{9,10},{10,1... | collective-permute-start | bytes 2162696 | tf_op jit(solution)/shard_map/ppermute | solution.py:17
  83.3 25.0 %collective-permute-start.7 = (bf16[256,1408]{1,0:T(8,128)(2,1)S(1)}, bf16[256,1408]{1,0:T(8,128)(2,1)S(1)}, u32[]{:S(2)}, u32[]{:S(2)}) collective-permute-start(bf16[256,1408]{1,0:T(8,128)(2,1)S(1)} %tick_1.1), channel_id=1, source_target_pairs={{0,4},{1,5},{2,6},{3,7},{4,11},{5,10},{6,9},{7,8},{16,20},{17,21},... | collective-permute-start | bytes 2162696 | tf_op jit(solution)/shard_map/ppermute | solution.py:17
  108.3 22.1 %collective-permute-start.6 = (bf16[256,1408]{1,0:T(8,128)(2,1)S(1)}, bf16[256,1408]{1,0:T(8,128)(2,1)S(1)}, u32[]{:S(2)}, u32[]{:S(2)}) collective-permute-start(bf16[256,1408]{1,0:T(8,128)(2,1)S(1)} %tick_2.1), channel_id=1, source_target_pairs={{0,1},{1,2},{2,3},{3,4},{4,5},{5,6},{6,7},{7,8},{8,9},{9,10},{10,1... | collective-permute-start | bytes 2162696 | tf_op jit(solution)/shard_map/ppermute | solution.py:17
  108.4 22.0 %collective-permute-start.8 = (bf16[256,1408]{1,0:T(8,128)(2,1)S(1)}, bf16[256,1408]{1,0:T(8,128)(2,1)S(1)}, u32[]{:S(2)}, u32[]{:S(2)}) collective-permute-start(bf16[256,1408]{1,0:T(8,128)(2,1)S(1)} %collective-permute-done.7), channel_id=1, source_target_pairs={{4,15},{5,14},{6,13},{7,12},{20,31},{21,30},{22,29},{23,28}} | collective-permute-start | bytes 2162696 | tf_op jit(solution)/shard_map/ppermute | solution.py:17

commit v4 on v1

v4 whole, which is shorter than its diff:
```python
import functools

import jax
import jax.numpy as jnp
from jax import lax
from jax.experimental import pallas as pl
from jax.experimental.pallas import tpu as pltpu
from jax.sharding import PartitionSpec as P

TICKS = 3


epsilon = 1e-06


def move(value, pairs, label):
    with jax.named_scope(label):
        return lax.ppermute(value, "section", pairs)


def spans(extent, step):
    return [(start, min(step, extent - start)) for start in range(0, extent, step)]


def start_one(copies, tests):
    section = lax.axis_index("section")
    for copy, test in zip(copies, tests):
        if test is None:
            copy.start()
        else:
            pl.when(test(section))(copy.start)


def row_pieces(source, target, sems, pieces):
    return [
        pltpu.make_async_copy(source.at[pl.ds(start, size), :], target.at[pl.ds(start, size), :], sems.at[i])
        for i, (start, size) in enumerate(pieces)
    ]


def column_pieces(source, target, sems, pieces):
    return [
        pltpu.make_async_copy(source.at[:, pl.ds(start, size)], target.at[:, pl.ds(start, size)], sems.at[i])
        for i, (start, size) in enumerate(pieces)
    ]


def dot(left, right):
    return jnp.dot(left, right, preferred_element_type=jnp.float32)


def block_kernel(*refs, tests, merge_pieces, pieces, fill):
    queues_hbm, refs = refs[: len(tests)], refs[len(tests) :]
    rows, gain, merging, upper, lower, out = refs[:6]
    rows_copies, merging_copies, upper_copies, lower_copies = [], [], [], []
    if fill:
        merging_hbm, upper_hbm, lower_hbm = merging, upper, lower
        rows_hbm, gain_hbm = rows, gain
        merging, upper, lower, queue, merged, total, queue_sem, rows, gain, rows_sem, merging_sem, upper_sem, lower_sem = refs[6:]
        rows_copies = [
            pltpu.make_async_copy(rows_hbm, rows, rows_sem.at[0]), pltpu.make_async_copy(gain_hbm, gain, rows_sem.at[1])
        ]
        merging_copies = row_pieces(merging_hbm, merging, merging_sem, merge_pieces)
        upper_copies = column_pieces(upper_hbm, upper, upper_sem, pieces)
        lower_copies = row_pieces(lower_hbm, lower, lower_sem, pieces)
    else:
        queue, merged, total, queue_sem = refs[6:]
    decoder = lax.axis_index("section") >= lax.axis_size("section") // 2
    width = rows.shape[1]
    queue_copies = [pltpu.make_async_copy(source, queue, queue_sem.at[0]) for source in queues_hbm]

    feed_copies = [copy for pair in zip(upper_copies, lower_copies) for copy in pair]
    window = 3

    def arrive(copies, number):
        if fill:
            copies[number].wait()
            if number + window < len(copies):
                copies[number + window].start()

    for copy in rows_copies:
        copy.start()

    @pl.when(decoder)
    def _():
        start_one(queue_copies, tests)
        for copy in (merging_copies + feed_copies)[:window]:
            copy.start()

    @pl.when(jnp.logical_not(decoder))
    def _():
        for copy in feed_copies[:window]:
            copy.start()

    for copy in rows_copies:
        copy.wait()

    @pl.when(decoder)
    def _():
        value = None
        for i, (start, size) in enumerate(merge_pieces):
            if start == width:
                queue_copies[0].wait()
            arrive(merging_copies + feed_copies[:window], i)
            source = rows if start < width else queue
            part = dot(source[:, pl.ds(start % width, size)], merging[pl.ds(start, size), :])
            value = part if value is None else value + part
        merged[...] = value

    @pl.when(jnp.logical_not(decoder))
    def _():
        merged[...] = rows[...].astype(jnp.float32)

    value = merged[...]
    center = jnp.mean(value, axis=1, keepdims=True)
    spread = jnp.mean(jnp.square(value - center), axis=1, keepdims=True)
    normed = ((value - center) * lax.rsqrt(spread + epsilon) * gain[...]).astype(jnp.bfloat16)
    for i, (start, size) in enumerate(pieces):
        arrive(feed_copies, 2 * i)
        raised = dot(normed, upper[:, pl.ds(start, size)])
        hidden = jax.nn.gelu(raised, approximate=True).astype(jnp.bfloat16)
        arrive(feed_copies, 2 * i + 1)
        part = dot(hidden, lower[pl.ds(start, size), :])
        if i == 0:
            total[...] = merged[...] + part
        elif i < len(pieces) - 1:
            total[...] += part
        else:
            out[...] = (total[...] + part).astype(out.dtype)


def block(rows, queue_choices, weights, name, fill=False):
    gain, merging, upper, lower = weights
    row_count, width = rows.shape
    hidden = upper.shape[1]
    merge_step = 512 if fill else width
    step = 1024
    merge_pieces = [(base + start, size) for base in (0, width) for start, size in spans(width, merge_step)]
    pieces = spans(hidden, step)
    anywhere = pl.BlockSpec(memory_space=pl.ANY)
    resident = pl.BlockSpec(memory_space=pltpu.VMEM)
    far = pl.BlockSpec(memory_space=pltpu.HBM)
    if fill:
        queue_choices = [(test, pltpu.with_memory_space_constraint(array, pltpu.HBM)) for test, array in queue_choices]
        rows, gain, merging, upper, lower = (
            pltpu.with_memory_space_constraint(array, pltpu.HBM) for array in (rows, gain, merging, upper, lower)
        )
    output = jax.ShapeDtypeStruct((row_count, width), jnp.bfloat16)
    copied = [jax.ShapeDtypeStruct(array.shape, array.dtype) for array in (merging, upper, lower)]
    scratch = [
        pltpu.VMEM((row_count, width), jnp.bfloat16),
        pltpu.VMEM((row_count, width), jnp.float32),
        pltpu.VMEM((row_count, width), jnp.float32),
        pltpu.SemaphoreType.DMA((1,)),
    ]
    if fill:
        scratch += [pltpu.VMEM(rows.shape, rows.dtype), pltpu.VMEM(gain.shape, gain.dtype)]
        scratch += [pltpu.SemaphoreType.DMA((len(some),)) for some in ((rows, gain), merge_pieces, pieces, pieces)]
    return pl.pallas_call(
        functools.partial(
            block_kernel, tests=[test for test, _ in queue_choices], merge_pieces=merge_pieces, pieces=pieces, fill=fill
        ),
        out_shape=[output, *copied] if fill else output,
        in_specs=[anywhere] * len(queue_choices) + [far if fill else resident] * 5,
        out_specs=[resident] * 4 if fill else resident,
        scratch_shapes=scratch,
        compiler_params=pltpu.CompilerParams(vmem_limit_bytes=(16 if fill else 12) * 1024 * 1024),
        cost_estimate=pl.CostEstimate(
            flops=2 * row_count * width * (2 * width + 2 * hidden),
            bytes_accessed=2 * (2 * width * width + 2 * width * hidden + 3 * row_count * width),
            transcendentals=row_count * hidden,
        ),
        name=name,
    )(*(array for _, array in queue_choices), rows, gain, merging, upper, lower)


def local(latent_rows, skip_queue, norm_gain, skip_weight, up_weight, down_weight):
    count = lax.axis_size("section")
    half = count // 2
    quarter = half // 2
    section = lax.axis_index("section")
    weights = (norm_gain, skip_weight[0], up_weight[0], down_weight[0])
    step_on = [(source, (source + 1) % count) for source in range(count)]
    by_hand = [quarter + source for source in range(quarter - 2)] + [half - 1, half - 2]
    handed = list(zip(range(quarter), by_hand))
    direct = [(source, count - 1 - source) for source in range(quarter, half)]
    passed = [(hand, count - 1 - source) for source, hand in handed]
    is_near = lambda section: section < half + quarter
    is_far = lambda section: section >= half + quarter

    late, shifted = 0, quarter - 2
    handed_first = [pair for pair in handed if pair[0] not in (late, shifted)] + [(shifted, quarter)]
    passed_first = [(hand, count - 1 - source) for source, hand in handed_first]
    handed_late = [(late, quarter)]
    passed_late = [(quarter, count - 1 - late)]
    is_late = lambda section: section == count - 1 - late
    is_far_else = lambda section: jnp.logical_and(is_far(section), jnp.logical_not(is_late(section)))

    arrived = move(skip_queue[0], handed + direct, "skip_0_near")
    output, *held = block(latent_rows[0], [(None, skip_queue[0])], weights, "tick_0", fill=True)
    weights = (norm_gain, *held)
    rows = move(output, step_on, "rows_0")
    output, arrived = lax.optimization_barrier((output, arrived))
    passed_0 = move(arrived, passed, "skip_0_far")
    arriving = move(output, handed_first + direct, "skip_1_near")
    arriving_late = move(output, handed_late, "skip_1_late")

    output = block(rows, [(is_near, arrived), (is_far, passed_0)], weights, "tick_1")
    passed_1 = move(arriving, passed_first, "skip_1_far")
    late_1 = move(arriving_late, passed_late, "skip_1_last")
    queue = [(is_near, arriving), (is_far_else, passed_1), (is_late, late_1)]
    rows = move(output, step_on, "rows_1")
    arrived = move(output, handed + direct, "skip_2_near")

    output = block(rows, queue, weights, "tick_2")
    rows = move(output, step_on, "rows_2")
    far = move(arrived, passed, "skip_2_far")
    queue_now = jnp.where(section >= half, jnp.where(is_far(section), far, arrived), output)
    return (rows[None], queue_now[None])


def solution(mesh):
    return jax.shard_map(
        local,
        mesh=mesh,
        in_specs=(
            P(("groups", "section"), None, None),
            P(("groups", "section"), None, None),
            P("section", None),
            P("section", None, None),
            P("section", None, None),
            P("section", None, None),
        ),
        out_specs=(P(("groups", "section"), None, None), P(("groups", "section"), None, None)),
        check_vma=False,
    )
```

time: 151 us -> 120 us (0.79)
  the two profiles are of different devices: /device:TPU:16 before, /device:TPU:31 now
where the time goes in v4:
time: 120 us
  waiting for transfers between devices  79.1 us (66%)
  Pallas kernels  30.7 us (26%)
  starting transfers between devices  7.59 us (6%)
    ppermute x11, waiting for transfers between devices, move(): return lax.ppermute(value, 'section', pairs)  79.1 us
    pallas_call x3, Pallas kernels, block(): pl.pallas_call(functools.partial(block_kernel, tests=[test for test, _ in...  30.7 us
    ppermute x11, starting transfers between devices, move(): return lax.ppermute(value, 'section', pairs)  7.59 us
  transfers between devices with their start and end apart: 11, of which 6 were waited for; matrix products, arithmetic and copies ran while one was open for 0% of the time, Pallas kernels for 26%

profile of v4, /device:TPU:31, one launch (start us, length us, event | category | flops | bytes accessed | tf_op | source)
XLA Modules:
  0.0 120.0 jit_solution(17782441979438100681)
XLA Ops:
  0.6 0.7 collective-permute-start
  1.3 0.0 copy-start
  1.4 12.5 %tick_0.1 = (bf16[256,1408]{1,0:T(8,128)(2,1)S(1)}, bf16[2816,1408]{1,0:T(8,128)(2,1)S(1)}, bf16[1408,3072]{1,0:T(8,128)(2,1)S(1)}, bf16[3072,1408]{1,0:T(8,128)(2,1)S(1)}) custom-call(bf16[256,1408]{1,0:T(8,128)(2,1)} %bitcast.13, bf16[256,1408]{1,0:T(8,128)(2,1)} %bitcast.11, f32[1,1408]{1,0:T(1,128)} %refs_4_.1, bf16[2816,1408]{1,0:T(8,128)(2,1)} %bitcast.10, ...), custom_call_target="tpu_custom_call" | custom-call | flops 6459228160 | bytes 27394048 | tf_op jit(solution)/shard_map/tick_0/pallas_call | solution.py:159
  13.8 0.1 collective-permute-start.6
  13.9 0.0 collective-permute-done.refs_0_
  13.9 1.3 %collective-permute-start.5 = (bf16[256,1408]{1,0:T(8,128)(2,1)S(1)}, bf16[256,1408]{1,0:T(8,128)(2,1)S(1)}, u32[]{:S(2)}, u32[]{:S(2)}) collective-permute-start(bf16[256,1408]{1,0:T(8,128)(2,1)S(1)} %collective-permute-done.refs_0_), channel_id=1, source_target_pairs={{4,15},{5,14},{7,13},{6,12},{20,31},{21,30},{23,29},{22,28}} | collective-permute-start | bytes 2162696 | tf_op jit(solution)/shard_map/skip_0_far/ppermute | solution.py:18
  15.2 0.7 collective-permute-start.1
  15.9 0.7 collective-permute-start.3
  16.7 5.5 %collective-permute-done.6.refs_2_ = bf16[256,1408]{1,0:T(8,128)(2,1)S(1)} collective-permute-done((bf16[256,1408]{1,0:T(8,128)(2,1)S(1)}, bf16[256,1408]{1,0:T(8,128)(2,1)S(1)}, u32[]{:S(2)}, u32[]{:S(2)}) %collective-permute-start.6) | collective-permute-done | bytes 720928 | tf_op jit(solution)/shard_map/rows_0/ppermute | solution.py:18
  22.1 17.7 %collective-permute-done.5.refs_1_ = bf16[256,1408]{1,0:T(8,128)(2,1)S(1)} collective-permute-done((bf16[256,1408]{1,0:T(8,128)(2,1)S(1)}, bf16[256,1408]{1,0:T(8,128)(2,1)S(1)}, u32[]{:S(2)}, u32[]{:S(2)}) %collective-permute-start.5) | collective-permute-done | bytes 720928 | tf_op jit(solution)/shard_map/skip_0_far/ppermute | solution.py:18
  39.8 0.0 copy-done
  39.8 9.1 %tick_1.1 = bf16[256,1408]{1,0:T(8,128)(2,1)S(1)} custom-call(bf16[256,1408]{1,0:T(8,128)(2,1)S(1)} %collective-permute-done.refs_0_, bf16[256,1408]{1,0:T(8,128)(2,1)S(1)} %collective-permute-done.5.refs_1_, bf16[256,1408]{1,0:T(8,128)(2,1)S(1)} %collective-permute-done.6.refs_2_, f32[1,1408]{1,0:T(1,128)S(1)} %copy-done, ...), custom_call_target="tpu_custom_call" | custom-call | flops 6459228160 | bytes 27394048 | tf_op jit(solution)/shard_map/tick_1/pallas_call | solution.py:159
  48.9 0.1 collective-permute-start.7
  49.0 0.0 collective-permute-done.1.refs_0_
  49.0 0.7 collective-permute-start.2
  49.7 0.0 collective-permute-done.3
  49.7 1.3 %collective-permute-start.4 = (bf16[256,1408]{1,0:T(8,128)(2,1)S(1)}, bf16[256,1408]{1,0:T(8,128)(2,1)S(1)}, u32[]{:S(2)}, u32[]{:S(2)}) collective-permute-start(bf16[256,1408]{1,0:T(8,128)(2,1)S(1)} %collective-permute-done.3), channel_id=1, source_target_pairs={{4,15},{20,31}} | collective-permute-start | bytes 2162696 | tf_op jit(solution)/shard_map/skip_1_last/ppermute | solution.py:18
  51.0 0.7 collective-permute-start.9
  51.8 5.5 %collective-permute-done.7.refs_3_ = bf16[256,1408]{1,0:T(8,128)(2,1)S(1)} collective-permute-done((bf16[256,1408]{1,0:T(8,128)(2,1)S(1)}, bf16[256,1408]{1,0:T(8,128)(2,1)S(1)}, u32[]{:S(2)}, u32[]{:S(2)}) %collective-permute-start.7) | collective-permute-done | bytes 720928 | tf_op jit(solution)/shard_map/rows_1/ppermute | solution.py:18
  57.2 0.0 collective-permute-done.2.refs_1_
  57.2 29.7 %collective-permute-done.4.refs_2_ = bf16[256,1408]{1,0:T(8,128)(2,1)S(1)} collective-permute-done((bf16[256,1408]{1,0:T(8,128)(2,1)S(1)}, bf16[256,1408]{1,0:T(8,128)(2,1)S(1)}, u32[]{:S(2)}, u32[]{:S(2)}) %collective-permute-start.4) | collective-permute-done | bytes 720928 | tf_op jit(solution)/shard_map/skip_1_last/ppermute | solution.py:18
  86.9 9.1 %tick_2.1 = bf16[256,1408]{1,0:T(8,128)(2,1)S(1)} custom-call(bf16[256,1408]{1,0:T(8,128)(2,1)S(1)} %collective-permute-done.1.refs_0_, bf16[256,1408]{1,0:T(8,128)(2,1)S(1)} %collective-permute-done.2.refs_1_, bf16[256,1408]{1,0:T(8,128)(2,1)S(1)} %collective-permute-done.4.refs_2_, bf16[256,1408]{1,0:T(8,128)(2,1)S(1)} %collective-permute-done.7.refs_3_, ...), custom_call_target="tpu_custom_call" | custom-call | flops 6459228160 | bytes 27394048 | tf_op jit(solution)/shard_map/tick_2/pallas_call | solution.py:159
  96.1 0.1 collective-permute-start.8
  96.2 0.0 collective-permute-done.9
  96.2 1.3 %collective-permute-start.10 = (bf16[256,1408]{1,0:T(8,128)(2,1)S(1)}, bf16[256,1408]{1,0:T(8,128)(2,1)S(1)}, u32[]{:S(2)}, u32[]{:S(2)}) collective-permute-start(bf16[256,1408]{1,0:T(8,128)(2,1)S(1)} %collective-permute-done.9), channel_id=1, source_target_pairs={{4,15},{5,14},{7,13},{6,12},{20,31},{21,30},{23,29},{22,28}} | collective-permute-start | bytes 2162696 | tf_op jit(solution)/shard_map/skip_2_far/ppermute | solution.py:18
  97.5 6.9 %collective-permute-done.8 = bf16[256,1408]{1,0:T(8,128)(2,1)S(1)} collective-permute-done((bf16[256,1408]{1,0:T(8,128)(2,1)S(1)}, bf16[256,1408]{1,0:T(8,128)(2,1)S(1)}, u32[]{:S(2)}, u32[]{:S(2)}) %collective-permute-start.8) | collective-permute-done | bytes 720928 | tf_op jit(solution)/shard_map/rows_2/ppermute | solution.py:18
  104.4 13.8 %collective-permute-done.10 = bf16[256,1408]{1,0:T(8,128)(2,1)S(1)} collective-permute-done((bf16[256,1408]{1,0:T(8,128)(2,1)S(1)}, bf16[256,1408]{1,0:T(8,128)(2,1)S(1)}, u32[]{:S(2)}, u32[]{:S(2)}) %collective-permute-start.10) | collective-permute-done | bytes 720928 | tf_op jit(solution)/shard_map/skip_2_far/ppermute | solution.py:18
  118.2 1.0 select_bitcast_fusion
  119.1 0.9 copy.9
Async XLA Ops:
  0.6 13.3 %collective-permute-start = (bf16[256,1408]{1,0:T(8,128)(2,1)}, bf16[256,1408]{1,0:T(8,128)(2,1)S(1)}, u32[]{:S(2)}, u32[]{:S(2)}) collective-permute-start(bf16[256,1408]{1,0:T(8,128)(2,1)} %bitcast.12), channel_id=1, source_target_pairs={{0,4},{1,5},{2,7},{3,6},{4,11},{5,10},{6,9},{7,8},{16,20},{17,21},... | collective-permute-start | bytes 2162696 | tf_op jit(solution)/shard_map/skip_0_near/ppermute | solution.py:18
  1.3 38.5 %copy-start = (f32[1,1408]{1,0:T(1,128)S(1)}, f32[1,1408]{1,0:T(1,128)}, u32[]{:S(2)}) copy-start(f32[1,1408]{1,0:T(1,128)} %refs_4_.1) | copy-start | bytes 16900
  13.8 8.3 %collective-permute-start.6 = (bf16[256,1408]{1,0:T(8,128)(2,1)S(1)}, bf16[256,1408]{1,0:T(8,128)(2,1)S(1)}, u32[]{:S(2)}, u32[]{:S(2)}) collective-permute-start(bf16[256,1408]{1,0:T(8,128)(2,1)S(1)} %get-tuple-element.9), channel_id=1, source_target_pairs={{0,1},{1,2},{2,3},{3,4},{4,5},{5,6},{6,7},{7,8},{8,9},{9,10},{10,1... | collective-permute-start | bytes 2162696 | tf_op jit(solution)/shard_map/rows_0/ppermute | solution.py:18
  13.9 25.9 %collective-permute-start.5 = (bf16[256,1408]{1,0:T(8,128)(2,1)S(1)}, bf16[256,1408]{1,0:T(8,128)(2,1)S(1)}, u32[]{:S(2)}, u32[]{:S(2)}) collective-permute-start(bf16[256,1408]{1,0:T(8,128)(2,1)S(1)} %collective-permute-done.refs_0_), channel_id=1, source_target_pairs={{4,15},{5,14},{7,13},{6,12},{20,31},{21,30},{23,29},{22,28}} | collective-permute-start | bytes 2162696 | tf_op jit(solution)/shard_map/skip_0_far/ppermute | solution.py:18
  15.2 33.8 %collective-permute-start.1 = (bf16[256,1408]{1,0:T(8,128)(2,1)S(1)}, bf16[256,1408]{1,0:T(8,128)(2,1)S(1)}, u32[]{:S(2)}, u32[]{:S(2)}) collective-permute-start(bf16[256,1408]{1,0:T(8,128)(2,1)S(1)} %get-tuple-element.9), channel_id=1, source_target_pairs={{1,5},{3,6},{2,4},{4,11},{5,10},{6,9},{7,8},{17,21},{19,22},{18,20... | collective-permute-start | bytes 2162696 | tf_op jit(solution)/shard_map/skip_1_near/ppermute | solution.py:18
  15.9 33.8 %collective-permute-start.3 = (bf16[256,1408]{1,0:T(8,128)(2,1)S(1)}, bf16[256,1408]{1,0:T(8,128)(2,1)S(1)}, u32[]{:S(2)}, u32[]{:S(2)}) collective-permute-start(bf16[256,1408]{1,0:T(8,128)(2,1)S(1)} %get-tuple-element.9), channel_id=1, source_target_pairs={{0,4},{16,20}} | collective-permute-start | bytes 2162696 | tf_op jit(solution)/shard_map/skip_1_late/ppermute | solution.py:18
  48.9 8.3 %collective-permute-start.7 = (bf16[256,1408]{1,0:T(8,128)(2,1)S(1)}, bf16[256,1408]{1,0:T(8,128)(2,1)S(1)}, u32[]{:S(2)}, u32[]{:S(2)}) collective-permute-start(bf16[256,1408]{1,0:T(8,128)(2,1)S(1)} %tick_1.1), channel_id=1, source_target_pairs={{0,1},{1,2},{2,3},{3,4},{4,5},{5,6},{6,7},{7,8},{8,9},{9,10},{10,1... | collective-permute-start | bytes 2162696 | tf_op jit(solution)/shard_map/rows_1/ppermute | solution.py:18
  49.0 8.2 %collective-permute-start.2 = (bf16[256,1408]{1,0:T(8,128)(2,1)S(1)}, bf16[256,1408]{1,0:T(8,128)(2,1)S(1)}, u32[]{:S(2)}, u32[]{:S(2)}) collective-permute-start(bf16[256,1408]{1,0:T(8,128)(2,1)S(1)} %collective-permute-done.1.refs_0_), channel_id=1, source_target_pairs={{5,14},{6,12},{4,13},{21,30},{22,28},{20,29}} | collective-permute-start | bytes 2162696 | tf_op jit(solution)/shard_map/skip_1_far/ppermute | solution.py:18
  49.7 37.2 %collective-permute-start.4 = (bf16[256,1408]{1,0:T(8,128)(2,1)S(1)}, bf16[256,1408]{1,0:T(8,128)(2,1)S(1)}, u32[]{:S(2)}, u32[]{:S(2)}) collective-permute-start(bf16[256,1408]{1,0:T(8,128)(2,1)S(1)} %collective-permute-done.3), channel_id=1, source_target_pairs={{4,15},{20,31}} | collective-permute-start | bytes 2162696 | tf_op jit(solution)/shard_map/skip_1_last/ppermute | solution.py:18
  51.0 45.1 %collective-permute-start.9 = (bf16[256,1408]{1,0:T(8,128)(2,1)S(1)}, bf16[256,1408]{1,0:T(8,128)(2,1)S(1)}, u32[]{:S(2)}, u32[]{:S(2)}) collective-permute-start(bf16[256,1408]{1,0:T(8,128)(2,1)S(1)} %tick_1.1), channel_id=1, source_target_pairs={{0,4},{1,5},{2,7},{3,6},{4,11},{5,10},{6,9},{7,8},{16,20},{17,21},... | collective-permute-start | bytes 2162696 | tf_op jit(solution)/shard_map/skip_2_near/ppermute | solution.py:18
  96.1 8.3 %collective-permute-start.8 = (bf16[256,1408]{1,0:T(8,128)(2,1)S(1)}, bf16[256,1408]{1,0:T(8,128)(2,1)S(1)}, u32[]{:S(2)}, u32[]{:S(2)}) collective-permute-start(bf16[256,1408]{1,0:T(8,128)(2,1)S(1)} %tick_2.1), channel_id=1, source_target_pairs={{0,1},{1,2},{2,3},{3,4},{4,5},{5,6},{6,7},{7,8},{8,9},{9,10},{10,1... | collective-permute-start | bytes 2162696 | tf_op jit(solution)/shard_map/rows_2/ppermute | solution.py:18
  96.2 22.0 %collective-permute-start.10 = (bf16[256,1408]{1,0:T(8,128)(2,1)S(1)}, bf16[256,1408]{1,0:T(8,128)(2,1)S(1)}, u32[]{:S(2)}, u32[]{:S(2)}) collective-permute-start(bf16[256,1408]{1,0:T(8,128)(2,1)S(1)} %collective-permute-done.9), channel_id=1, source_target_pairs={{4,15},{5,14},{7,13},{6,12},{20,31},{21,30},{23,29},{22,28}} | collective-permute-start | bytes 2162696 | tf_op jit(solution)/shard_map/skip_2_far/ppermute | solution.py:18

commit v5 on v4

--- a/solution.py
+++ b/solution.py
@@ -22,13 +22,18 @@
     return [(start, min(step, extent - start)) for start in range(0, extent, step)]
 
 
-def start_one(copies, tests):
+def start_one(choices, tests):
     section = lax.axis_index("section")
-    for copy, test in zip(copies, tests):
+
+    def start(copies):
+        for copy in copies:
+            copy.start()
+
+    for copies, (test, _) in zip(choices, tests):
         if test is None:
-            copy.start()
+            start(copies)
         else:
-            pl.when(test(section))(copy.start)
+            pl.when(test(section))(functools.partial(start, copies))
 
 
 def row_pieces(source, target, sems, pieces):
@@ -50,7 +55,8 @@
 
 
 def block_kernel(*refs, tests, merge_pieces, pieces, fill):
-    queues_hbm, refs = refs[: len(tests)], refs[len(tests) :]
+    count = sum(number for _, number in tests)
+    queues_hbm, refs = refs[:count], refs[count:]
     rows, gain, merging, upper, lower, out = refs[:6]
     rows_copies, merging_copies, upper_copies, lower_copies = [], [], [], []
     if fill:
@@ -67,7 +73,18 @@
         queue, merged, total, queue_sem = refs[6:]
     decoder = lax.axis_index("section") >= lax.axis_size("section") // 2
     width = rows.shape[1]
-    queue_copies = [pltpu.make_async_copy(source, queue, queue_sem.at[0]) for source in queues_hbm]
+    top = queue.shape[0] // 2
+    halves = [(0, top), (top, queue.shape[0] - top)]
+    queue_copies = []
+    for test, number in tests:
+        sources, queues_hbm = queues_hbm[:number], queues_hbm[number:]
+        parts = [sources[0].at[pl.ds(start, size), :] for start, size in halves] if number == 1 else sources
+        queue_copies.append(
+            [
+                pltpu.make_async_copy(part, queue.at[pl.ds(start, size), :], queue_sem.at[i])
+                for i, (part, (start, size)) in enumerate(zip(parts, halves))
+            ]
+        )
 
     feed_copies = [copy for pair in zip(upper_copies, lower_copies) for copy in pair]
     window = 3
@@ -100,7 +117,8 @@
         value = None
         for i, (start, size) in enumerate(merge_pieces):
             if start == width:
-                queue_copies[0].wait()
+                for copy in queue_copies[0]:
+                    copy.wait()
             arrive(merging_copies + feed_copies[:window], i)
             source = rows if start < width else queue
             part = dot(source[:, pl.ds(start % width, size)], merging[pl.ds(start, size), :])
@@ -131,6 +149,8 @@
 
 def block(rows, queue_choices, weights, name, fill=False):
     gain, merging, upper, lower = weights
+    queue_choices = [(test, arrays if isinstance(arrays, list) else [arrays]) for test, arrays in queue_choices]
+    operand_count = sum(len(arrays) for _, arrays in queue_choices)
     row_count, width = rows.shape
     hidden = upper.shape[1]
     merge_step = 512 if fill else width
@@ -141,7 +161,10 @@
     resident = pl.BlockSpec(memory_space=pltpu.VMEM)
     far = pl.BlockSpec(memory_space=pltpu.HBM)
     if fill:
-        queue_choices = [(test, pltpu.with_memory_space_constraint(array, pltpu.HBM)) for test, array in queue_choices]
+        queue_choices = [
+            (test, [pltpu.with_memory_space_constraint(array, pltpu.HBM) for array in arrays])
+            for test, arrays in queue_choices
+        ]
         rows, gain, merging, upper, lower = (
             pltpu.with_memory_space_constraint(array, pltpu.HBM) for array in (rows, gain, merging, upper, lower)
         )
@@ -151,17 +174,17 @@
         pltpu.VMEM((row_count, width), jnp.bfloat16),
         pltpu.VMEM((row_count, width), jnp.float32),
         pltpu.VMEM((row_count, width), jnp.float32),
-        pltpu.SemaphoreType.DMA((1,)),
+        pltpu.SemaphoreType.DMA((2,)),
     ]
     if fill:
         scratch += [pltpu.VMEM(rows.shape, rows.dtype), pltpu.VMEM(gain.shape, gain.dtype)]
         scratch += [pltpu.SemaphoreType.DMA((len(some),)) for some in ((rows, gain), merge_pieces, pieces, pieces)]
     return pl.pallas_call(
         functools.partial(
-            block_kernel, tests=[test for test, _ in queue_choices], merge_pieces=merge_pieces, pieces=pieces, fill=fill
+            block_kernel, tests=[(test, len(arrays)) for test, arrays in queue_choices], merge_pieces=merge_pieces, pieces=pieces, fill=fill
         ),
         out_shape=[output, *copied] if fill else output,
-        in_specs=[anywhere] * len(queue_choices) + [far if fill else resident] * 5,
+        in_specs=[anywhere] * operand_count + [far if fill else resident] * 5,
         out_specs=[resident] * 4 if fill else resident,
         scratch_shapes=scratch,
         compiler_params=pltpu.CompilerParams(vmem_limit_bytes=(16 if fill else 12) * 1024 * 1024),
@@ -171,7 +194,7 @@
             transcendentals=row_count * hidden,
         ),
         name=name,
-    )(*(array for _, array in queue_choices), rows, gain, merging, upper, lower)
+    )(*(array for _, arrays in queue_choices for array in arrays), rows, gain, merging, upper, lower)
 
 
 def local(latent_rows, skip_queue, norm_gain, skip_weight, up_weight, down_weight):
@@ -181,20 +204,16 @@
     section = lax.axis_index("section")
     weights = (norm_gain, skip_weight[0], up_weight[0], down_weight[0])
     step_on = [(source, (source + 1) % count) for source in range(count)]
-    by_hand = [quarter + source for source in range(quarter - 2)] + [half - 1, half - 2]
-    handed = list(zip(range(quarter), by_hand))
+    handed = [(source, half - 1 - source) for source in range(quarter)]
     direct = [(source, count - 1 - source) for source in range(quarter, half)]
     passed = [(hand, count - 1 - source) for source, hand in handed]
     is_near = lambda section: section < half + quarter
     is_far = lambda section: section >= half + quarter
-
-    late, shifted = 0, quarter - 2
-    handed_first = [pair for pair in handed if pair[0] not in (late, shifted)] + [(shifted, quarter)]
-    passed_first = [(hand, count - 1 - source) for source, hand in handed_first]
-    handed_late = [(late, quarter)]
-    passed_late = [(quarter, count - 1 - late)]
-    is_late = lambda section: section == count - 1 - late
-    is_far_else = lambda section: jnp.logical_and(is_far(section), jnp.logical_not(is_late(section)))
+    split = [(0, (quarter, quarter + 1)), (1, (half - 2, half - 1))]
+    handed_half = [[(source, hands[part]) for source, hands in split] for part in (0, 1)]
+    passed_half = [[(hands[part], count - 1 - source) for source, hands in split] for part in (0, 1)]
+    is_split = lambda section: section >= count - len(split)
+    is_whole = lambda section: jnp.logical_and(is_far(section), jnp.logical_not(is_split(section)))
 
     arrived = move(skip_queue[0], handed + direct, "skip_0_near")
     output, *held = block(latent_rows[0], [(None, skip_queue[0])], weights, "tick_0", fill=True)
@@ -202,13 +221,14 @@
     rows = move(output, step_on, "rows_0")
     output, arrived = lax.optimization_barrier((output, arrived))
     passed_0 = move(arrived, passed, "skip_0_far")
-    arriving = move(output, handed_first + direct, "skip_1_near")
-    arriving_late = move(output, handed_late, "skip_1_late")
+    arriving = move(output, handed[len(split) :] + direct, "skip_1_near")
+    top = output.shape[0] // 2
+    halves = [move(part, pairs, "skip_1_halves") for part, pairs in zip((output[:top], output[top:]), handed_half)]
 
     output = block(rows, [(is_near, arrived), (is_far, passed_0)], weights, "tick_1")
-    passed_1 = move(arriving, passed_first, "skip_1_far")
-    late_1 = move(arriving_late, passed_late, "skip_1_last")
-    queue = [(is_near, arriving), (is_far_else, passed_1), (is_late, late_1)]
+    passed_1 = move(arriving, passed[len(split) :], "skip_1_far")
+    halves = [move(part, pairs, "skip_1_far_halves") for part, pairs in zip(halves, passed_half)]
+    queue = [(is_near, arriving), (is_whole, passed_1), (is_split, halves)]
     rows = move(output, step_on, "rows_1")
     arrived = move(output, handed + direct, "skip_2_near")
 

time: 120 us -> 116 us (0.967)
  waiting for transfers between devices: 79.1 us -> 71.2 us
  starting transfers between devices: 7.59 us -> 10.5 us
    ppermute x11 -> x13, waiting for transfers between devices: 79.1 us -> 71.2 us  [move(): return lax.ppermute(value, 'section', pairs)]
    ppermute x11 -> x13, starting transfers between devices: 7.59 us -> 10.5 us  [move(): return lax.ppermute(value, 'section', pairs)]
  transfers between devices with their start and end apart: 11 -> 13, of which waited for: 6 -> 5; matrix products, arithmetic and copies ran while one was open for 0% -> 0% of each run, Pallas kernels for 26% -> 27%
where the time goes in v5:
time: 116 us
  waiting for transfers between devices  71.2 us (61%)
  Pallas kernels  31.2 us (27%)
  starting transfers between devices  10.5 us (9%)
    ppermute x13, waiting for transfers between devices, move(): return lax.ppermute(value, 'section', pairs)  71.2 us
    pallas_call x3, Pallas kernels, block(): pl.pallas_call(functools.partial(block_kernel, tests=[(test, len(arrays))...  31.2 us
    ppermute x13, starting transfers between devices, move(): return lax.ppermute(value, 'section', pairs)  10.5 us
  transfers between devices with their start and end apart: 13, of which 5 were waited for; matrix products, arithmetic and copies ran while one was open for 0% of the time, Pallas kernels for 27%

profile of v5, /device:TPU:31, one launch (start us, length us, event | category | flops | bytes accessed | tf_op | source)
XLA Modules:
  0.0 115.5 jit_solution(736257353508484650)
XLA Ops:
  0.6 0.7 collective-permute-start
  1.3 0.0 copy-start
  1.4 12.9 %tick_0.1 = (bf16[256,1408]{1,0:T(8,128)(2,1)S(1)}, bf16[2816,1408]{1,0:T(8,128)(2,1)S(1)}, bf16[1408,3072]{1,0:T(8,128)(2,1)S(1)}, bf16[3072,1408]{1,0:T(8,128)(2,1)S(1)}) custom-call(bf16[256,1408]{1,0:T(8,128)(2,1)} %bitcast.13, bf16[256,1408]{1,0:T(8,128)(2,1)} %bitcast.11, f32[1,1408]{1,0:T(1,128)} %refs_5_.1, bf16[2816,1408]{1,0:T(8,128)(2,1)} %bitcast.10, ...), custom_call_target="tpu_custom_call" | custom-call | flops 6459228160 | bytes 27394048 | tf_op jit(solution)/shard_map/tick_0/pallas_call | solution.py:182
  14.3 1.0 collective-permute-start.8
  15.3 0.0 collective-permute-done.refs_0_
  15.3 1.3 %collective-permute-start.7 = (bf16[256,1408]{1,0:T(8,128)(2,1)S(1)}, bf16[256,1408]{1,0:T(8,128)(2,1)S(1)}, u32[]{:S(2)}, u32[]{:S(2)}) collective-permute-start(bf16[256,1408]{1,0:T(8,128)(2,1)S(1)} %collective-permute-done.refs_0_), channel_id=1, source_target_pairs={{7,15},{6,14},{5,13},{4,12},{23,31},{22,30},{21,29},{20,28}} | collective-permute-start | bytes 2162696 | tf_op jit(solution)/shard_map/skip_0_far/ppermute | solution.py:18
  16.5 0.7 collective-permute-start.1
  17.3 0.1 fusion
  17.3 0.7 collective-permute-start.3
  18.0 0.7 collective-permute-start.5
  18.7 4.8 %collective-permute-done.8.refs_2_ = bf16[256,1408]{1,0:T(8,128)(2,1)S(1)} collective-permute-done((bf16[256,1408]{1,0:T(8,128)(2,1)S(1)}, bf16[256,1408]{1,0:T(8,128)(2,1)S(1)}, u32[]{:S(2)}, u32[]{:S(2)}) %collective-permute-start.8) | collective-permute-done | bytes 720928 | tf_op jit(solution)/shard_map/rows_0/ppermute | solution.py:18
  23.5 24.0 %collective-permute-done.7.refs_1_ = bf16[256,1408]{1,0:T(8,128)(2,1)S(1)} collective-permute-done((bf16[256,1408]{1,0:T(8,128)(2,1)S(1)}, bf16[256,1408]{1,0:T(8,128)(2,1)S(1)}, u32[]{:S(2)}, u32[]{:S(2)}) %collective-permute-start.7) | collective-permute-done | bytes 720928 | tf_op jit(solution)/shard_map/skip_0_far/ppermute | solution.py:18
  47.5 0.0 copy-done
  47.5 9.1 %tick_1.1 = bf16[256,1408]{1,0:T(8,128)(2,1)S(1)} custom-call(bf16[256,1408]{1,0:T(8,128)(2,1)S(1)} %collective-permute-done.refs_0_, bf16[256,1408]{1,0:T(8,128)(2,1)S(1)} %collective-permute-done.7.refs_1_, bf16[256,1408]{1,0:T(8,128)(2,1)S(1)} %collective-permute-done.8.refs_2_, f32[1,1408]{1,0:T(1,128)S(1)} %copy-done, ...), custom_call_target="tpu_custom_call" | custom-call | flops 6459228160 | bytes 27394048 | tf_op jit(solution)/shard_map/tick_1/pallas_call | solution.py:182
  56.6 0.1 collective-permute-start.9
  56.7 0.0 collective-permute-done.1.refs_0_
  56.7 0.7 collective-permute-start.2
  57.4 0.0 collective-permute-done.3
  57.4 1.3 %collective-permute-start.4 = (bf16[128,1408]{1,0:T(8,128)(2,1)S(1)}, bf16[128,1408]{1,0:T(8,128)(2,1)S(1)}, u32[]{:S(2)}, u32[]{:S(2)}) collective-permute-start(bf16[128,1408]{1,0:T(8,128)(2,1)S(1)} %collective-permute-done.3), channel_id=1, source_target_pairs={{4,15},{6,14},{20,31},{22,30}} | collective-permute-start | bytes 1081352 | tf_op jit(solution)/shard_map/skip_1_far_halves/ppermute | solution.py:18
  58.7 0.0 collective-permute-done.5
  58.7 1.3 %collective-permute-start.6 = (bf16[128,1408]{1,0:T(8,128)(2,1)S(1)}, bf16[128,1408]{1,0:T(8,128)(2,1)S(1)}, u32[]{:S(2)}, u32[]{:S(2)}) collective-permute-start(bf16[128,1408]{1,0:T(8,128)(2,1)S(1)} %collective-permute-done.5), channel_id=1, source_target_pairs={{5,15},{7,14},{21,31},{23,30}} | collective-permute-start | bytes 1081352 | tf_op jit(solution)/shard_map/skip_1_far_halves/ppermute | solution.py:18
  60.0 0.7 collective-permute-start.11
  60.8 20.3 %collective-permute-done.4.refs_2_ = bf16[128,1408]{1,0:T(8,128)(2,1)S(1)} collective-permute-done((bf16[128,1408]{1,0:T(8,128)(2,1)S(1)}, bf16[128,1408]{1,0:T(8,128)(2,1)S(1)}, u32[]{:S(2)}, u32[]{:S(2)}) %collective-permute-start.4) | collective-permute-done | bytes 360480 | tf_op jit(solution)/shard_map/skip_1_far_halves/ppermute | solution.py:18
  81.0 0.0 collective-permute-done.6.refs_3_
  81.0 0.0 collective-permute-done.9.refs_4_
  81.0 0.0 collective-permute-done.2.refs_1_
  81.0 9.2 %tick_2.1 = bf16[256,1408]{1,0:T(8,128)(2,1)S(1)} custom-call(bf16[256,1408]{1,0:T(8,128)(2,1)S(1)} %collective-permute-done.1.refs_0_, bf16[256,1408]{1,0:T(8,128)(2,1)S(1)} %collective-permute-done.2.refs_1_, bf16[128,1408]{1,0:T(8,128)(2,1)S(1)} %collective-permute-done.4.refs_2_, bf16[128,1408]{1,0:T(8,128)(2,1)S(1)} %collective-permute-done.6.refs_3_, ...), custom_call_target="tpu_custom_call" | custom-call | flops 6459228160 | bytes 27394048 | tf_op jit(solution)/shard_map/tick_2/pallas_call | solution.py:182
  90.2 0.1 collective-permute-start.10
  90.3 0.0 collective-permute-done.11
  90.3 1.3 %collective-permute-start.12 = (bf16[256,1408]{1,0:T(8,128)(2,1)S(1)}, bf16[256,1408]{1,0:T(8,128)(2,1)S(1)}, u32[]{:S(2)}, u32[]{:S(2)}) collective-permute-start(bf16[256,1408]{1,0:T(8,128)(2,1)S(1)} %collective-permute-done.11), channel_id=1, source_target_pairs={{7,15},{6,14},{5,13},{4,12},{23,31},{22,30},{21,29},{20,28}} | collective-permute-start | bytes 2162696 | tf_op jit(solution)/shard_map/skip_2_far/ppermute | solution.py:18
  91.6 6.9 %collective-permute-done.10 = bf16[256,1408]{1,0:T(8,128)(2,1)S(1)} collective-permute-done((bf16[256,1408]{1,0:T(8,128)(2,1)S(1)}, bf16[256,1408]{1,0:T(8,128)(2,1)S(1)}, u32[]{:S(2)}, u32[]{:S(2)}) %collective-permute-start.10) | collective-permute-done | bytes 720928 | tf_op jit(solution)/shard_map/rows_2/ppermute | solution.py:18
  98.5 15.2 %collective-permute-done.12 = bf16[256,1408]{1,0:T(8,128)(2,1)S(1)} collective-permute-done((bf16[256,1408]{1,0:T(8,128)(2,1)S(1)}, bf16[256,1408]{1,0:T(8,128)(2,1)S(1)}, u32[]{:S(2)}, u32[]{:S(2)}) %collective-permute-start.12) | collective-permute-done | bytes 720928 | tf_op jit(solution)/shard_map/skip_2_far/ppermute | solution.py:18
  113.7 1.0 select_bitcast_fusion
  114.6 0.9 copy.9
Async XLA Ops:
  0.6 14.6 %collective-permute-start = (bf16[256,1408]{1,0:T(8,128)(2,1)}, bf16[256,1408]{1,0:T(8,128)(2,1)S(1)}, u32[]{:S(2)}, u32[]{:S(2)}) collective-permute-start(bf16[256,1408]{1,0:T(8,128)(2,1)} %bitcast.12), channel_id=1, source_target_pairs={{0,7},{1,6},{2,5},{3,4},{4,11},{5,10},{6,9},{7,8},{16,23},{17,22},... | collective-permute-start | bytes 2162696 | tf_op jit(solution)/shard_map/skip_0_near/ppermute | solution.py:18
  1.3 46.2 %copy-start = (f32[1,1408]{1,0:T(1,128)S(1)}, f32[1,1408]{1,0:T(1,128)}, u32[]{:S(2)}) copy-start(f32[1,1408]{1,0:T(1,128)} %refs_5_.1) | copy-start | bytes 16900
  14.3 9.2 %collective-permute-start.8 = (bf16[256,1408]{1,0:T(8,128)(2,1)S(1)}, bf16[256,1408]{1,0:T(8,128)(2,1)S(1)}, u32[]{:S(2)}, u32[]{:S(2)}) collective-permute-start(bf16[256,1408]{1,0:T(8,128)(2,1)S(1)} %get-tuple-element.9), channel_id=1, source_target_pairs={{0,1},{1,2},{2,3},{3,4},{4,5},{5,6},{6,7},{7,8},{8,9},{9,10},{10,1... | collective-permute-start | bytes 2162696 | tf_op jit(solution)/shard_map/rows_0/ppermute | solution.py:18
  15.3 32.3 %collective-permute-start.7 = (bf16[256,1408]{1,0:T(8,128)(2,1)S(1)}, bf16[256,1408]{1,0:T(8,128)(2,1)S(1)}, u32[]{:S(2)}, u32[]{:S(2)}) collective-permute-start(bf16[256,1408]{1,0:T(8,128)(2,1)S(1)} %collective-permute-done.refs_0_), channel_id=1, source_target_pairs={{7,15},{6,14},{5,13},{4,12},{23,31},{22,30},{21,29},{20,28}} | collective-permute-start | bytes 2162696 | tf_op jit(solution)/shard_map/skip_0_far/ppermute | solution.py:18
  16.5 40.2 %collective-permute-start.1 = (bf16[256,1408]{1,0:T(8,128)(2,1)S(1)}, bf16[256,1408]{1,0:T(8,128)(2,1)S(1)}, u32[]{:S(2)}, u32[]{:S(2)}) collective-permute-start(bf16[256,1408]{1,0:T(8,128)(2,1)S(1)} %get-tuple-element.9), channel_id=1, source_target_pairs={{2,5},{3,4},{4,11},{5,10},{6,9},{7,8},{18,21},{19,20},{20,27},{21,... | collective-permute-start | bytes 2162696 | tf_op jit(solution)/shard_map/skip_1_near/ppermute | solution.py:18
  17.3 40.1 %collective-permute-start.3 = (bf16[128,1408]{1,0:T(8,128)(2,1)S(1)}, bf16[128,1408]{1,0:T(8,128)(2,1)S(1)}, u32[]{:S(2)}, u32[]{:S(2)}) collective-permute-start(bf16[128,1408]{1,0:T(8,128)(2,1)S(1)} %get-tuple-element.15), channel_id=1, source_target_pairs={{0,4},{1,6},{16,20},{17,22}} | collective-permute-start | bytes 1081352 | tf_op jit(solution)/shard_map/skip_1_halves/ppermute | solution.py:18
  18.0 40.7 %collective-permute-start.5 = (bf16[128,1408]{1,0:T(8,128)(2,1)S(1)}, bf16[128,1408]{1,0:T(8,128)(2,1)S(1)}, u32[]{:S(2)}, u32[]{:S(2)}) collective-permute-start(bf16[128,1408]{1,0:T(8,128)(2,1)S(1)} %get-tuple-element.14), channel_id=1, source_target_pairs={{0,5},{1,7},{16,21},{17,23}} | collective-permute-start | bytes 1081352 | tf_op jit(solution)/shard_map/skip_1_halves/ppermute | solution.py:18
  56.6 24.4 %collective-permute-start.9 = (bf16[256,1408]{1,0:T(8,128)(2,1)S(1)}, bf16[256,1408]{1,0:T(8,128)(2,1)S(1)}, u32[]{:S(2)}, u32[]{:S(2)}) collective-permute-start(bf16[256,1408]{1,0:T(8,128)(2,1)S(1)} %tick_1.1), channel_id=1, source_target_pairs={{0,1},{1,2},{2,3},{3,4},{4,5},{5,6},{6,7},{7,8},{8,9},{9,10},{10,1... | collective-permute-start | bytes 2162696 | tf_op jit(solution)/shard_map/rows_1/ppermute | solution.py:18
  56.7 24.3 %collective-permute-start.2 = (bf16[256,1408]{1,0:T(8,128)(2,1)S(1)}, bf16[256,1408]{1,0:T(8,128)(2,1)S(1)}, u32[]{:S(2)}, u32[]{:S(2)}) collective-permute-start(bf16[256,1408]{1,0:T(8,128)(2,1)S(1)} %collective-permute-done.1.refs_0_), channel_id=1, source_target_pairs={{5,13},{4,12},{21,29},{20,28}} | collective-permute-start | bytes 2162696 | tf_op jit(solution)/shard_map/skip_1_far/ppermute | solution.py:18
  57.4 23.6 %collective-permute-start.4 = (bf16[128,1408]{1,0:T(8,128)(2,1)S(1)}, bf16[128,1408]{1,0:T(8,128)(2,1)S(1)}, u32[]{:S(2)}, u32[]{:S(2)}) collective-permute-start(bf16[128,1408]{1,0:T(8,128)(2,1)S(1)} %collective-permute-done.3), channel_id=1, source_target_pairs={{4,15},{6,14},{20,31},{22,30}} | collective-permute-start | bytes 1081352 | tf_op jit(solution)/shard_map/skip_1_far_halves/ppermute | solution.py:18
  58.7 22.3 %collective-permute-start.6 = (bf16[128,1408]{1,0:T(8,128)(2,1)S(1)}, bf16[128,1408]{1,0:T(8,128)(2,1)S(1)}, u32[]{:S(2)}, u32[]{:S(2)}) collective-permute-start(bf16[128,1408]{1,0:T(8,128)(2,1)S(1)} %collective-permute-done.5), channel_id=1, source_target_pairs={{5,15},{7,14},{21,31},{23,30}} | collective-permute-start | bytes 1081352 | tf_op jit(solution)/shard_map/skip_1_far_halves/ppermute | solution.py:18
  60.0 30.2 %collective-permute-start.11 = (bf16[256,1408]{1,0:T(8,128)(2,1)S(1)}, bf16[256,1408]{1,0:T(8,128)(2,1)S(1)}, u32[]{:S(2)}, u32[]{:S(2)}) collective-permute-start(bf16[256,1408]{1,0:T(8,128)(2,1)S(1)} %tick_1.1), channel_id=1, source_target_pairs={{0,7},{1,6},{2,5},{3,4},{4,11},{5,10},{6,9},{7,8},{16,23},{17,22},... | collective-permute-start | bytes 2162696 | tf_op jit(solution)/shard_map/skip_2_near/ppermute | solution.py:18
  90.2 8.3 %collective-permute-start.10 = (bf16[256,1408]{1,0:T(8,128)(2,1)S(1)}, bf16[256,1408]{1,0:T(8,128)(2,1)S(1)}, u32[]{:S(2)}, u32[]{:S(2)}) collective-permute-start(bf16[256,1408]{1,0:T(8,128)(2,1)S(1)} %tick_2.1), channel_id=1, source_target_pairs={{0,1},{1,2},{2,3},{3,4},{4,5},{5,6},{6,7},{7,8},{8,9},{9,10},{10,1... | collective-permute-start | bytes 2162696 | tf_op jit(solution)/shard_map/rows_2/ppermute | solution.py:18
  90.3 23.4 %collective-permute-start.12 = (bf16[256,1408]{1,0:T(8,128)(2,1)S(1)}, bf16[256,1408]{1,0:T(8,128)(2,1)S(1)}, u32[]{:S(2)}, u32[]{:S(2)}) collective-permute-start(bf16[256,1408]{1,0:T(8,128)(2,1)S(1)} %collective-permute-done.11), channel_id=1, source_target_pairs={{7,15},{6,14},{5,13},{4,12},{23,31},{22,30},{21,29},{20,28}} | collective-permute-start | bytes 2162696 | tf_op jit(solution)/shard_map/skip_2_far/ppermute | solution.py:18

commit v6 on v5

--- a/solution.py
+++ b/solution.py
@@ -11,6 +11,7 @@
 
 
 epsilon = 1e-06
+CUT = 4
 
 
 def move(value, pairs, label):
@@ -73,16 +74,16 @@
         queue, merged, total, queue_sem = refs[6:]
     decoder = lax.axis_index("section") >= lax.axis_size("section") // 2
     width = rows.shape[1]
-    top = queue.shape[0] // 2
-    halves = [(0, top), (top, queue.shape[0] - top)]
+    cut = queue.shape[0] // CUT
+    pieces_of = [(0, cut), (cut, queue.shape[0] - cut)]
     queue_copies = []
     for test, number in tests:
         sources, queues_hbm = queues_hbm[:number], queues_hbm[number:]
-        parts = [sources[0].at[pl.ds(start, size), :] for start, size in halves] if number == 1 else sources
+        parts = [sources[0].at[pl.ds(start, size), :] for start, size in pieces_of] if number == 1 else sources
         queue_copies.append(
             [
                 pltpu.make_async_copy(part, queue.at[pl.ds(start, size), :], queue_sem.at[i])
-                for i, (part, (start, size)) in enumerate(zip(parts, halves))
+                for i, (part, (start, size)) in enumerate(zip(parts, pieces_of))
             ]
         )
 
@@ -197,6 +198,27 @@
     )(*(array for _, arrays in queue_choices for array in arrays), rows, gain, merging, upper, lower)
 
 
+def place_kernel(*refs, tests):
+    sources, out, sem = refs[: len(tests)], refs[-2], refs[-1]
+    copies = [pltpu.make_async_copy(source, out.at[0], sem.at[0]) for source in sources]
+    start_one([[copy] for copy in copies], [(test, 1) for test in tests])
+    copies[0].wait()
+
+
+def place(choices, name, after=()):
+    shape, dtype = choices[0][1].shape, choices[0][1].dtype
+    anywhere = pl.BlockSpec(memory_space=pl.ANY)
+    return pl.pallas_call(
+        functools.partial(place_kernel, tests=[test for test, _ in choices]),
+        out_shape=jax.ShapeDtypeStruct((1, *shape), dtype),
+        in_specs=[pl.BlockSpec(memory_space=pltpu.VMEM)] * len(choices) + [anywhere] * len(after),
+        out_specs=anywhere,
+        scratch_shapes=[pltpu.SemaphoreType.DMA((1,))],
+        compiler_params=pltpu.CompilerParams(vmem_limit_bytes=1024 * 1024),
+        name=name,
+    )(*(array for _, array in choices), *(pltpu.with_memory_space_constraint(array, pltpu.HBM) for array in after))
+
+
 def local(latent_rows, skip_queue, norm_gain, skip_weight, up_weight, down_weight):
     count = lax.axis_size("section")
     half = count // 2
@@ -209,34 +231,40 @@
     passed = [(hand, count - 1 - source) for source, hand in handed]
     is_near = lambda section: section < half + quarter
     is_far = lambda section: section >= half + quarter
-    split = [(0, (quarter, quarter + 1)), (1, (half - 2, half - 1))]
-    handed_half = [[(source, hands[part]) for source, hands in split] for part in (0, 1)]
-    passed_half = [[(hands[part], count - 1 - source) for source, hands in split] for part in (0, 1)]
+    split = [(0, (quarter, quarter + 1)), (1, (quarter + 1, half - 2))]
+    handed_piece = [[(source, hands[part]) for source, hands in split] for part in (0, 1)]
+    passed_piece = [[(hands[part], count - 1 - source) for source, hands in split] for part in (0, 1)]
     is_split = lambda section: section >= count - len(split)
     is_whole = lambda section: jnp.logical_and(is_far(section), jnp.logical_not(is_split(section)))
-
-    arrived = move(skip_queue[0], handed + direct, "skip_0_near")
-    output, *held = block(latent_rows[0], [(None, skip_queue[0])], weights, "tick_0", fill=True)
+    top = latent_rows.shape[1] // CUT
+
+    skip = skip_queue[0]
+    near = move(skip, handed + direct, "skip_0_near")
+    output, *held = block(latent_rows[0], [(None, skip)], weights, "tick_0", fill=True)
     weights = (norm_gain, *held)
     rows = move(output, step_on, "rows_0")
-    output, arrived = lax.optimization_barrier((output, arrived))
-    passed_0 = move(arrived, passed, "skip_0_far")
-    arriving = move(output, handed[len(split) :] + direct, "skip_1_near")
-    top = output.shape[0] // 2
-    halves = [move(part, pairs, "skip_1_halves") for part, pairs in zip((output[:top], output[top:]), handed_half)]
-
-    output = block(rows, [(is_near, arrived), (is_far, passed_0)], weights, "tick_1")
-    passed_1 = move(arriving, passed[len(split) :], "skip_1_far")
-    halves = [move(part, pairs, "skip_1_far_halves") for part, pairs in zip(halves, passed_half)]
-    queue = [(is_near, arriving), (is_whole, passed_1), (is_split, halves)]
+    output, near = lax.optimization_barrier((output, near))
+    queue = [(is_near, near), (is_far, move(near, passed, "skip_0_far"))]
+    near = move(output, direct, "skip_1_near")
+    hand = move(output, handed[len(split) :], "skip_1_handed")
+    pieces = [move(part, pairs, "skip_1_pieces") for part, pairs in zip((output[:top], output[top:]), handed_piece)]
+
+    output = block(rows, queue, weights, "tick_1")
+    far = move(hand, passed[len(split) :], "skip_1_far")
+    pieces = [move(part, pairs, "skip_1_far_pieces") for part, pairs in zip(pieces, passed_piece)]
+    queue = [(is_near, near), (is_whole, far), (is_split, pieces)]
     rows = move(output, step_on, "rows_1")
-    arrived = move(output, handed + direct, "skip_2_near")
+    near = move(output, handed + direct, "skip_2_near")
 
     output = block(rows, queue, weights, "tick_2")
     rows = move(output, step_on, "rows_2")
-    far = move(arrived, passed, "skip_2_far")
-    queue_now = jnp.where(section >= half, jnp.where(is_far(section), far, arrived), output)
-    return (rows[None], queue_now[None])
+    far = move(near, passed, "skip_2_far")
+    is_encoder = lambda section: section < half
+    is_near_decoder = lambda section: jnp.logical_and(section >= half, is_near(section))
+    next_rows = place([(None, rows)], "place_rows")
+    choices = [(is_encoder, output), (is_near_decoder, near), (is_far, far)]
+    next_queue = place(choices, "place_queue", after=(next_rows,))
+    return (next_rows, next_queue)
 
 
 def solution(mesh):

time: 116 us -> 114 us (0.983)
  the two profiles are of different devices: /device:TPU:31 before, /device:TPU:27 now
where the time goes in v6:
time: 114 us
  waiting for transfers between devices  50.9 us (45%)
  Pallas kernels  32.8 us (29%)
  starting transfers between devices  29 us (25%)
    ppermute x14, waiting for transfers between devices, move(): return lax.ppermute(value, 'section', pairs)  50.9 us
    pallas_call x3, Pallas kernels, block(): pl.pallas_call(functools.partial(block_kernel, tests=[(test, len(arrays))...  31.1 us
    ppermute x14, starting transfers between devices, move(): return lax.ppermute(value, 'section', pairs)  29 us
  transfers between devices with their start and end apart: 14, of which 6 were waited for; matrix products, arithmetic and copies ran while one was open for 0% of the time, Pallas kernels for 28%

profile of v6, /device:TPU:27, one launch (start us, length us, event | category | flops | bytes accessed | tf_op | source)
XLA Modules:
  0.0 113.8 jit_solution(11763834168303629827)
XLA Ops:
  0.6 0.7 collective-permute-start
  1.3 0.0 copy-start
  1.4 12.9 %tick_0.1 = (bf16[256,1408]{1,0:T(8,128)(2,1)S(1)}, bf16[2816,1408]{1,0:T(8,128)(2,1)S(1)}, bf16[1408,3072]{1,0:T(8,128)(2,1)S(1)}, bf16[3072,1408]{1,0:T(8,128)(2,1)S(1)}) custom-call(bf16[256,1408]{1,0:T(8,128)(2,1)} %bitcast.10, bf16[256,1408]{1,0:T(8,128)(2,1)} %bitcast.8, f32[1,1408]{1,0:T(1,128)} %refs_5_.1, bf16[2816,1408]{1,0:T(8,128)(2,1)} %bitcast.7, ...), custom_call_target="tpu_custom_call" | custom-call | flops 6459228160 | bytes 27394048 | tf_op jit(solution)/shard_map/tick_0/pallas_call | solution.py:183
  14.2 1.8 %collective-permute-start.9 = (bf16[256,1408]{1,0:T(8,128)(2,1)S(1)}, bf16[256,1408]{1,0:T(8,128)(2,1)S(1)}, u32[]{:S(2)}, u32[]{:S(2)}) collective-permute-start(bf16[256,1408]{1,0:T(8,128)(2,1)S(1)} %get-tuple-element.9), channel_id=1, source_target_pairs={{0,1},{1,2},{2,3},{3,4},{4,5},{5,6},{6,7},{7,8},{8,9},{9,10},{10,1... | collective-permute-start | bytes 2162696 | tf_op jit(solution)/shard_map/rows_0/ppermute | solution.py:19
  16.1 0.0 collective-permute-done.refs_0_
  16.1 1.3 %collective-permute-start.8 = (bf16[256,1408]{1,0:T(8,128)(2,1)S(1)}, bf16[256,1408]{1,0:T(8,128)(2,1)S(1)}, u32[]{:S(2)}, u32[]{:S(2)}) collective-permute-start(bf16[256,1408]{1,0:T(8,128)(2,1)S(1)} %collective-permute-done.refs_0_), channel_id=1, source_target_pairs={{7,15},{6,14},{5,13},{4,12},{23,31},{22,30},{21,29},{20,28}} | collective-permute-start | bytes 2162696 | tf_op jit(solution)/shard_map/skip_0_far/ppermute | solution.py:19
  17.4 0.7 collective-permute-start.2
  18.1 0.7 collective-permute-start.1
  18.8 0.7 collective-permute-start.6
  19.5 4.8 %collective-permute-done.9.refs_2_ = bf16[256,1408]{1,0:T(8,128)(2,1)S(1)} collective-permute-done((bf16[256,1408]{1,0:T(8,128)(2,1)S(1)}, bf16[256,1408]{1,0:T(8,128)(2,1)S(1)}, u32[]{:S(2)}, u32[]{:S(2)}) %collective-permute-start.9) | collective-permute-done | bytes 720928 | tf_op jit(solution)/shard_map/rows_0/ppermute | solution.py:19
  24.3 15.6 %collective-permute-done.8.refs_1_ = bf16[256,1408]{1,0:T(8,128)(2,1)S(1)} collective-permute-done((bf16[256,1408]{1,0:T(8,128)(2,1)S(1)}, bf16[256,1408]{1,0:T(8,128)(2,1)S(1)}, u32[]{:S(2)}, u32[]{:S(2)}) %collective-permute-start.8) | collective-permute-done | bytes 720928 | tf_op jit(solution)/shard_map/skip_0_far/ppermute | solution.py:19
  39.9 0.0 copy-done
  39.9 9.1 %tick_1.1 = bf16[256,1408]{1,0:T(8,128)(2,1)S(1)} custom-call(bf16[256,1408]{1,0:T(8,128)(2,1)S(1)} %collective-permute-done.refs_0_, bf16[256,1408]{1,0:T(8,128)(2,1)S(1)} %collective-permute-done.8.refs_1_, bf16[256,1408]{1,0:T(8,128)(2,1)S(1)} %collective-permute-done.9.refs_2_, f32[1,1408]{1,0:T(1,128)S(1)} %copy-done, ...), custom_call_target="tpu_custom_call" | custom-call | flops 6459228160 | bytes 27394048 | tf_op jit(solution)/shard_map/tick_1/pallas_call | solution.py:183
  49.0 2.8 %collective-permute-start.10 = (bf16[256,1408]{1,0:T(8,128)(2,1)S(1)}, bf16[256,1408]{1,0:T(8,128)(2,1)S(1)}, u32[]{:S(2)}, u32[]{:S(2)}) collective-permute-start(bf16[256,1408]{1,0:T(8,128)(2,1)S(1)} %tick_1.1), channel_id=1, source_target_pairs={{0,1},{1,2},{2,3},{3,4},{4,5},{5,6},{6,7},{7,8},{8,9},{9,10},{10,1... | collective-permute-start | bytes 2162696 | tf_op jit(solution)/shard_map/rows_1/ppermute | solution.py:19
  51.8 0.0 collective-permute-done.2
  51.8 1.3 %collective-permute-start.3 = (bf16[256,1408]{1,0:T(8,128)(2,1)S(1)}, bf16[256,1408]{1,0:T(8,128)(2,1)S(1)}, u32[]{:S(2)}, u32[]{:S(2)}) collective-permute-start(bf16[256,1408]{1,0:T(8,128)(2,1)S(1)} %collective-permute-done.2), channel_id=1, source_target_pairs={{5,13},{4,12},{21,29},{20,28}} | collective-permute-start | bytes 2162696 | tf_op jit(solution)/shard_map/skip_1_far/ppermute | solution.py:19
  53.0 0.0 collective-permute-done.6
  53.1 0.7 collective-permute-start.7
  53.8 0.7 collective-permute-start.4
  54.5 0.0 collective-permute-done.4
  54.5 0.7 collective-permute-start.5
  55.2 0.0 collective-permute-done.5.refs_2_
  55.2 0.7 collective-permute-start.12
  55.9 0.0 collective-permute-done.1.refs_0_
  55.9 0.0 collective-permute-done.7.refs_3_
  55.9 4.1 %collective-permute-done.10.refs_4_ = bf16[256,1408]{1,0:T(8,128)(2,1)S(1)} collective-permute-done((bf16[256,1408]{1,0:T(8,128)(2,1)S(1)}, bf16[256,1408]{1,0:T(8,128)(2,1)S(1)}, u32[]{:S(2)}, u32[]{:S(2)}) %collective-permute-start.10) | collective-permute-done | bytes 720928 | tf_op jit(solution)/shard_map/rows_1/ppermute | solution.py:19
  60.0 12.4 %collective-permute-done.3.refs_1_ = bf16[256,1408]{1,0:T(8,128)(2,1)S(1)} collective-permute-done((bf16[256,1408]{1,0:T(8,128)(2,1)S(1)}, bf16[256,1408]{1,0:T(8,128)(2,1)S(1)}, u32[]{:S(2)}, u32[]{:S(2)}) %collective-permute-start.3) | collective-permute-done | bytes 720928 | tf_op jit(solution)/shard_map/skip_1_far/ppermute | solution.py:19
  72.4 9.1 %tick_2.1.refs_0_ = bf16[256,1408]{1,0:T(8,128)(2,1)S(1)} custom-call(bf16[256,1408]{1,0:T(8,128)(2,1)S(1)} %collective-permute-done.1.refs_0_, bf16[256,1408]{1,0:T(8,128)(2,1)S(1)} %collective-permute-done.3.refs_1_, bf16[64,1408]{1,0:T(8,128)(2,1)S(1)} %collective-permute-done.5.refs_2_, bf16[192,1408]{1,0:T(8,128)(2,1)S(1)} %collective-permute-done.7.refs_3_, ...), custom_call_target="tpu_custom_call" | custom-call | flops 6459228160 | bytes 27394048 | tf_op jit(solution)/shard_map/tick_2/pallas_call | solution.py:183
  81.5 15.0 %collective-permute-start.11 = (bf16[256,1408]{1,0:T(8,128)(2,1)S(1)}, bf16[256,1408]{1,0:T(8,128)(2,1)S(1)}, u32[]{:S(2)}, u32[]{:S(2)}) collective-permute-start(bf16[256,1408]{1,0:T(8,128)(2,1)S(1)} %tick_2.1.refs_0_), channel_id=1, source_target_pairs={{0,1},{1,2},{2,3},{3,4},{4,5},{5,6},{6,7},{7,8},{8,9},{9,10},{10,1... | collective-permute-start | bytes 2162696 | tf_op jit(solution)/shard_map/rows_2/ppermute | solution.py:19
  96.5 0.0 collective-permute-done.12.refs_1_
  96.5 1.3 %collective-permute-start.13 = (bf16[256,1408]{1,0:T(8,128)(2,1)S(1)}, bf16[256,1408]{1,0:T(8,128)(2,1)S(1)}, u32[]{:S(2)}, u32[]{:S(2)}) collective-permute-start(bf16[256,1408]{1,0:T(8,128)(2,1)S(1)} %collective-permute-done.12.refs_1_), channel_id=1, source_target_pairs={{7,15},{6,14},{5,13},{4,12},{23,31},{22,30},{21,29},{20,28}} | collective-permute-start | bytes 2162696 | tf_op jit(solution)/shard_map/skip_2_far/ppermute | solution.py:19
  97.8 6.9 %collective-permute-done.11.refs_0_ = bf16[256,1408]{1,0:T(8,128)(2,1)S(1)} collective-permute-done((bf16[256,1408]{1,0:T(8,128)(2,1)S(1)}, bf16[256,1408]{1,0:T(8,128)(2,1)S(1)}, u32[]{:S(2)}, u32[]{:S(2)}) %collective-permute-start.11) | collective-permute-done | bytes 720928 | tf_op jit(solution)/shard_map/rows_2/ppermute | solution.py:19
  104.8 0.9 place_rows.1.refs_3_
  105.6 7.1 %collective-permute-done.13.refs_2_ = bf16[256,1408]{1,0:T(8,128)(2,1)S(1)} collective-permute-done((bf16[256,1408]{1,0:T(8,128)(2,1)S(1)}, bf16[256,1408]{1,0:T(8,128)(2,1)S(1)}, u32[]{:S(2)}, u32[]{:S(2)}) %collective-permute-start.13) | collective-permute-done | bytes 720928 | tf_op jit(solution)/shard_map/skip_2_far/ppermute | solution.py:19
  112.7 0.9 place_queue.1
  (2 shorter events, 0.1 us)
Async XLA Ops:
  0.6 15.4 %collective-permute-start = (bf16[256,1408]{1,0:T(8,128)(2,1)}, bf16[256,1408]{1,0:T(8,128)(2,1)S(1)}, u32[]{:S(2)}, u32[]{:S(2)}) collective-permute-start(bf16[256,1408]{1,0:T(8,128)(2,1)} %bitcast.9), channel_id=1, source_target_pairs={{0,7},{1,6},{2,5},{3,4},{4,11},{5,10},{6,9},{7,8},{16,23},{17,22},... | collective-permute-start | bytes 2162696 | tf_op jit(solution)/shard_map/skip_0_near/ppermute | solution.py:19
  1.3 38.6 %copy-start = (f32[1,1408]{1,0:T(1,128)S(1)}, f32[1,1408]{1,0:T(1,128)}, u32[]{:S(2)}) copy-start(f32[1,1408]{1,0:T(1,128)} %refs_5_.1) | copy-start | bytes 16900
  14.2 10.1 %collective-permute-start.9 = (bf16[256,1408]{1,0:T(8,128)(2,1)S(1)}, bf16[256,1408]{1,0:T(8,128)(2,1)S(1)}, u32[]{:S(2)}, u32[]{:S(2)}) collective-permute-start(bf16[256,1408]{1,0:T(8,128)(2,1)S(1)} %get-tuple-element.9), channel_id=1, source_target_pairs={{0,1},{1,2},{2,3},{3,4},{4,5},{5,6},{6,7},{7,8},{8,9},{9,10},{10,1... | collective-permute-start | bytes 2162696 | tf_op jit(solution)/shard_map/rows_0/ppermute | solution.py:19
  16.1 23.8 %collective-permute-start.8 = (bf16[256,1408]{1,0:T(8,128)(2,1)S(1)}, bf16[256,1408]{1,0:T(8,128)(2,1)S(1)}, u32[]{:S(2)}, u32[]{:S(2)}) collective-permute-start(bf16[256,1408]{1,0:T(8,128)(2,1)S(1)} %collective-permute-done.refs_0_), channel_id=1, source_target_pairs={{7,15},{6,14},{5,13},{4,12},{23,31},{22,30},{21,29},{20,28}} | collective-permute-start | bytes 2162696 | tf_op jit(solution)/shard_map/skip_0_far/ppermute | solution.py:19
  17.4 34.4 %collective-permute-start.2 = (bf16[256,1408]{1,0:T(8,128)(2,1)S(1)}, bf16[256,1408]{1,0:T(8,128)(2,1)S(1)}, u32[]{:S(2)}, u32[]{:S(2)}) collective-permute-start(bf16[256,1408]{1,0:T(8,128)(2,1)S(1)} %get-tuple-element.9), channel_id=1, source_target_pairs={{2,5},{3,4},{18,21},{19,20}} | collective-permute-start | bytes 2162696 | tf_op jit(solution)/shard_map/skip_1_handed/ppermute | solution.py:19
  18.1 37.8 %collective-permute-start.1 = (bf16[256,1408]{1,0:T(8,128)(2,1)S(1)}, bf16[256,1408]{1,0:T(8,128)(2,1)S(1)}, u32[]{:S(2)}, u32[]{:S(2)}) collective-permute-start(bf16[256,1408]{1,0:T(8,128)(2,1)S(1)} %get-tuple-element.9), channel_id=1, source_target_pairs={{4,11},{5,10},{6,9},{7,8},{20,27},{21,26},{22,25},{23,24}} | collective-permute-start | bytes 2162696 | tf_op jit(solution)/shard_map/skip_1_near/ppermute | solution.py:19
  18.8 34.2 %collective-permute-start.6 = (bf16[192,1408]{1,0:T(8,128)(2,1)S(1)}, bf16[192,1408]{1,0:T(8,128)(2,1)S(1)}, u32[]{:S(2)}, u32[]{:S(2)}) collective-permute-start(bf16[192,1408]{1,0:T(8,128)(2,1)S(1)} %slice.7), channel_id=1, source_target_pairs={{0,5},{1,6},{16,21},{17,22}} | collective-permute-start | bytes 1622024 | tf_op jit(solution)/shard_map/skip_1_pieces/ppermute | solution.py:19
  49.0 11.0 %collective-permute-start.10 = (bf16[256,1408]{1,0:T(8,128)(2,1)S(1)}, bf16[256,1408]{1,0:T(8,128)(2,1)S(1)}, u32[]{:S(2)}, u32[]{:S(2)}) collective-permute-start(bf16[256,1408]{1,0:T(8,128)(2,1)S(1)} %tick_1.1), channel_id=1, source_target_pairs={{0,1},{1,2},{2,3},{3,4},{4,5},{5,6},{6,7},{7,8},{8,9},{9,10},{10,1... | collective-permute-start | bytes 2162696 | tf_op jit(solution)/shard_map/rows_1/ppermute | solution.py:19
  51.8 20.6 %collective-permute-start.3 = (bf16[256,1408]{1,0:T(8,128)(2,1)S(1)}, bf16[256,1408]{1,0:T(8,128)(2,1)S(1)}, u32[]{:S(2)}, u32[]{:S(2)}) collective-permute-start(bf16[256,1408]{1,0:T(8,128)(2,1)S(1)} %collective-permute-done.2), channel_id=1, source_target_pairs={{5,13},{4,12},{21,29},{20,28}} | collective-permute-start | bytes 2162696 | tf_op jit(solution)/shard_map/skip_1_far/ppermute | solution.py:19
  53.1 2.8 %collective-permute-start.7 = (bf16[192,1408]{1,0:T(8,128)(2,1)S(1)}, bf16[192,1408]{1,0:T(8,128)(2,1)S(1)}, u32[]{:S(2)}, u32[]{:S(2)}) collective-permute-start(bf16[192,1408]{1,0:T(8,128)(2,1)S(1)} %collective-permute-done.6), channel_id=1, source_target_pairs={{5,15},{6,14},{21,31},{22,30}} | collective-permute-start | bytes 1622024 | tf_op jit(solution)/shard_map/skip_1_far_pieces/ppermute | solution.py:19
  53.8 0.7 collective-permute-start.4
  54.5 0.7 collective-permute-start.5
  55.2 41.4 %collective-permute-start.12 = (bf16[256,1408]{1,0:T(8,128)(2,1)S(1)}, bf16[256,1408]{1,0:T(8,128)(2,1)S(1)}, u32[]{:S(2)}, u32[]{:S(2)}) collective-permute-start(bf16[256,1408]{1,0:T(8,128)(2,1)S(1)} %tick_1.1), channel_id=1, source_target_pairs={{0,7},{1,6},{2,5},{3,4},{4,11},{5,10},{6,9},{7,8},{16,23},{17,22},... | collective-permute-start | bytes 2162696 | tf_op jit(solution)/shard_map/skip_2_near/ppermute | solution.py:19
  81.5 23.3 %collective-permute-start.11 = (bf16[256,1408]{1,0:T(8,128)(2,1)S(1)}, bf16[256,1408]{1,0:T(8,128)(2,1)S(1)}, u32[]{:S(2)}, u32[]{:S(2)}) collective-permute-start(bf16[256,1408]{1,0:T(8,128)(2,1)S(1)} %tick_2.1.refs_0_), channel_id=1, source_target_pairs={{0,1},{1,2},{2,3},{3,4},{4,5},{5,6},{6,7},{7,8},{8,9},{9,10},{10,1... | collective-permute-start | bytes 2162696 | tf_op jit(solution)/shard_map/rows_2/ppermute | solution.py:19
  96.5 16.2 %collective-permute-start.13 = (bf16[256,1408]{1,0:T(8,128)(2,1)S(1)}, bf16[256,1408]{1,0:T(8,128)(2,1)S(1)}, u32[]{:S(2)}, u32[]{:S(2)}) collective-permute-start(bf16[256,1408]{1,0:T(8,128)(2,1)S(1)} %collective-permute-done.12.refs_1_), channel_id=1, source_target_pairs={{7,15},{6,14},{5,13},{4,12},{23,31},{22,30},{21,29},{20,28}} | collective-permute-start | bytes 2162696 | tf_op jit(solution)/shard_map/skip_2_far/ppermute | solution.py:19
